TPU v7x, 32 devices: a whole 2x2x4 slice. The times are simulated.
32 devices in a mesh: seq: 8 (over z, y), tp: 4 (over x, core).
Axes of the slice: x: 2, y: 2, z: 4, core: 2. Of those that a mesh axis runs over, the one named last changes fastest.
Arguments:
- query_in: bfloat16 [1024, 1024], P('seq', 'tp'), may hold values from -6 to 6
- key_in: bfloat16 [1024, 1024], P('seq', 'tp'), may hold values from -6 to 6
- value_in: bfloat16 [1024, 1024], P('seq', 'tp'), may hold values from -6 to 6
- short_weight: float32 [3, 7, 1024], P(None, None, 'tp'), may hold values from -2 to 2
- residue: float32 [16, 1024], P(None, 'tp'), may hold values from -1.5 to 1.5
- rate: float32 [16, 1024], P(None, 'tp'), may hold values from 1e-05 to 0.05
- skip: float32 [1024], P('tp'), may hold values from -4 to 4
- out_weight: bfloat16 [1024, 4096], P('tp'), may hold values from -0.1875 to 0.1875
Outputs:
- mixed: bfloat16 [1024, 4096], P('seq', 'tp')
All inputs are finite; a program needn't handle non-finite values.
Results may differ from a plain program's by a relative error of at most 0.0049.
Values may be sent and summed in bfloat16 or wider, within the bound.
A program may use at most 64 MiB of HBM per device.

v0:
```python
import math

import jax
import jax.numpy as jnp
from jax import lax
from jax.sharding import PartitionSpec as P


def passed_along(block, axis, distance):
    devices = range(lax.axis_size(axis))
    route = [(i - distance, i) for i in devices if i - distance in devices]
    return lax.ppermute(block, axis, route)


def short_conv(signal, border, weights):
    taps = weights.shape[0]
    rows_here = signal.shape[0]
    padded = jnp.concatenate([border.astype(jnp.float32), signal.astype(jnp.float32)], axis=0)
    total = jnp.zeros((rows_here, signal.shape[1]), jnp.float32)
    for offset in range(taps):
        total = total + weights[offset] * padded[taps - 1 - offset : taps - 1 - offset + rows_here]
    return total


def modal_spectrum(angles, parity, rate_rows, residue_rows, length):
    half_sine = 2.0 * jnp.sin(0.5 * angles) ** 2
    full_sine = jnp.sin(angles)
    shape_out = (angles + parity + rate_rows[0]).shape
    spec_real = jnp.zeros(shape_out, jnp.float32)
    spec_imag = jnp.zeros(shape_out, jnp.float32)
    for order_index in range(rate_rows.shape[0]):
        decay = rate_rows[order_index]
        retain = jnp.exp(-decay)
        amplitude = residue_rows[order_index] * jnp.sqrt(-jnp.expm1(-2.0 * decay))
        leftover = jnp.exp(-decay * length)
        numerator = amplitude * (1.0 - leftover * parity)
        below_real = -jnp.expm1(-decay) + retain * half_sine
        below_imag = retain * full_sine
        below_norm = below_real * below_real + below_imag * below_imag
        spec_real = spec_real + numerator * below_real / below_norm
        spec_imag = spec_imag - numerator * below_imag / below_norm
    return (spec_real, spec_imag)


def local(query_in, key_in, value_in, short_weight, residue, rate, skip, out_weight):
    rows_dev, channels = query_in.shape
    shards = lax.axis_size("seq")
    own_index = lax.axis_index("seq")
    cols_dev = rows_dev // shards
    length = shards * rows_dev
    period = 2 * length
    precise = lax.Precision.HIGHEST
    taps = short_weight.shape[1]
    rims = passed_along(
        (
            query_in[rows_dev - taps + 1 :],
            key_in[rows_dev - taps + 1 :],
            value_in[rows_dev - taps + 1 :],
        ),
        "seq",
        1,
    )
    queries = short_conv(query_in, rims[0], short_weight[0])
    keys = short_conv(key_in, rims[1], short_weight[1])
    values = short_conv(value_in, rims[2], short_weight[2])
    gated = keys * values
    indices = jnp.arange(rows_dev, dtype=jnp.int32)
    inner_phase = (
        2.0
        * math.pi
        / rows_dev
        * (indices[:, None] * indices[None, :] % rows_dev).astype(jnp.float32)
    )
    dft_cos = jnp.cos(inner_phase)
    dft_sin = jnp.sin(inner_phase)
    columns = lax.all_to_all(
        gated.reshape(shards, cols_dev, channels), "seq", split_axis=0, concat_axis=0, tiled=True
    )
    spectral = jnp.arange(2 * shards, dtype=jnp.int32)
    sources = jnp.arange(shards, dtype=jnp.int32)
    outer_phase = (
        2.0
        * math.pi
        / (2 * shards)
        * (spectral[:, None] * sources[None, :] % (2 * shards)).astype(jnp.float32)
    )
    z_real = jnp.einsum("ap,psc->asc", jnp.cos(outer_phase), columns, precision=precise)
    z_imag = -jnp.einsum("ap,psc->asc", jnp.sin(outer_phase), columns, precision=precise)
    held_cols = own_index * cols_dev + jnp.arange(cols_dev, dtype=jnp.int32)
    twist = (
        2.0
        * math.pi
        / period
        * (spectral[:, None] * held_cols[None, :] % period).astype(jnp.float32)
    )[:, :, None]
    twist_cos = jnp.cos(twist)
    twist_sin = jnp.sin(twist)
    turned_real = z_real * twist_cos + z_imag * twist_sin
    turned_imag = z_imag * twist_cos - z_real * twist_sin
    moved_real, moved_imag = (
        lax.all_to_all(
            turned_real.reshape(shards, 2, cols_dev, channels),
            "seq",
            split_axis=0,
            concat_axis=2,
            tiled=True,
        ),
        lax.all_to_all(
            turned_imag.reshape(shards, 2, cols_dev, channels),
            "seq",
            split_axis=0,
            concat_axis=2,
            tiled=True,
        ),
    )
    moved_real = moved_real.reshape(2, rows_dev, channels)
    moved_imag = moved_imag.reshape(2, rows_dev, channels)
    x_real = jnp.einsum("bj,tjc->tbc", dft_cos, moved_real, precision=precise) + jnp.einsum(
        "bj,tjc->tbc", dft_sin, moved_imag, precision=precise
    )
    x_imag = jnp.einsum("bj,tjc->tbc", dft_cos, moved_imag, precision=precise) - jnp.einsum(
        "bj,tjc->tbc", dft_sin, moved_real, precision=precise
    )
    held_freq = 2 * own_index + jnp.arange(2, dtype=jnp.int32)
    frequency = held_freq[:, None] + 2 * shards * indices[None, :]
    angles = (2.0 * math.pi / period * frequency.astype(jnp.float32))[:, :, None]
    parity = (1 - 2 * (held_freq % 2)).astype(jnp.float32)[:, None, None]
    spec_real, spec_imag = modal_spectrum(angles, parity, rate, residue, length)
    y_real = x_real * spec_real - x_imag * spec_imag
    y_imag = x_real * spec_imag + x_imag * spec_real
    g_real = jnp.einsum("bj,tbc->tjc", dft_cos, y_real, precision=precise) - jnp.einsum(
        "bj,tbc->tjc", dft_sin, y_imag, precision=precise
    )
    g_imag = jnp.einsum("bj,tbc->tjc", dft_cos, y_imag, precision=precise) + jnp.einsum(
        "bj,tbc->tjc", dft_sin, y_real, precision=precise
    )
    back_phase = (
        2.0
        * math.pi
        / period
        * (held_freq[:, None] * indices[None, :] % period).astype(jnp.float32)
    )[:, :, None]
    back_cos = jnp.cos(back_phase)
    back_sin = jnp.sin(back_phase)
    w_real = g_real * back_cos - g_imag * back_sin
    w_imag = g_imag * back_cos + g_real * back_sin
    w_real, w_imag = (
        lax.all_to_all(
            w_real.reshape(2, shards, cols_dev, channels),
            "seq",
            split_axis=1,
            concat_axis=0,
            tiled=True,
        ),
        lax.all_to_all(
            w_imag.reshape(2, shards, cols_dev, channels),
            "seq",
            split_axis=1,
            concat_axis=0,
            tiled=True,
        ),
    )
    w_real = w_real.reshape(2 * shards, cols_dev, channels)
    w_imag = w_imag.reshape(2 * shards, cols_dev, channels)
    out_rows = jnp.arange(2 * shards, dtype=jnp.int32)
    row_phase = (
        2.0
        * math.pi
        / (2 * shards)
        * (out_rows[:, None] * spectral[None, :] % (2 * shards)).astype(jnp.float32)
    )
    row_cos = jnp.cos(row_phase)
    row_sin = jnp.sin(row_phase)
    out_real = jnp.einsum("pa,asc->psc", row_cos, w_real, precision=precise) - jnp.einsum(
        "pa,asc->psc", row_sin, w_imag, precision=precise
    )
    out_imag = jnp.einsum("pa,asc->psc", row_cos, w_imag, precision=precise) + jnp.einsum(
        "pa,asc->psc", row_sin, w_real, precision=precise
    )
    recv_real, recv_imag = (
        lax.all_to_all(
            out_real.reshape(2, shards, cols_dev, channels),
            "seq",
            split_axis=1,
            concat_axis=2,
            tiled=True,
        ),
        lax.all_to_all(
            out_imag.reshape(2, shards, cols_dev, channels),
            "seq",
            split_axis=1,
            concat_axis=2,
            tiled=True,
        ),
    )
    longconv = recv_real[0, 0] / period
    hyena = (queries * (longconv + skip * gated)).astype(jnp.bfloat16)
    partial_out = jnp.dot(hyena, out_weight, preferred_element_type=jnp.float32)
    return lax.psum_scatter(partial_out, "tp", scatter_dimension=1, tiled=True).astype(jnp.bfloat16)


def solution(mesh):
    in_specs = (
        P("seq", "tp"),
        P("seq", "tp"),
        P("seq", "tp"),
        P(None, None, "tp"),
        P(None, "tp"),
        P(None, "tp"),
        P("tp"),
        P("tp", None),
    )
    out_specs = P("seq", "tp")
    return jax.shard_map(local, mesh=mesh, in_specs=in_specs, out_specs=out_specs, check_vma=False)
```

profile of v0, /device:TPU:9, one launch (start us, length us, event | category | flops | bytes accessed | tf_op | source)
XLA Modules:
  0.0 149.2 jit_solution(8282748885274865695)
XLA Ops:
  7.4 3.1 %collective-permute-start.2 = (bf16[6,256]{1,0:T(8,128)(2,1)S(1)}, bf16[6,256]{1,0:T(8,128)(2,1)S(1)}, u32[]{:S(2)}, u32[]{:S(2)}) collective-permute-start(bf16[6,256]{1,0:T(8,128)(2,1)S(1)} %slice.302), channel_id=1, source_target_pairs={{0,4},{4,8},{8,12},{12,16},{16,20},{20,24},{24,28},{1,5},{5,9},{9,... | collective-permute-start | bytes 9224 | tf_op jit(solution)/shard_map/ppermute | solution.py:12
  11.2 3.1 %collective-permute-start.1 = (bf16[6,256]{1,0:T(8,128)(2,1)S(1)}, bf16[6,256]{1,0:T(8,128)(2,1)S(1)}, u32[]{:S(2)}, u32[]{:S(2)}) collective-permute-start(bf16[6,256]{1,0:T(8,128)(2,1)S(1)} %slice.288), channel_id=1, source_target_pairs={{0,4},{4,8},{8,12},{12,16},{16,20},{20,24},{24,28},{1,5},{5,9},{9,... | collective-permute-start | bytes 9224 | tf_op jit(solution)/shard_map/ppermute | solution.py:12
  14.4 0.9 multiply_exponential_fusion.3
  15.2 1.0 multiply_exponential_fusion.15
  16.3 1.0 exponential-minus-one_negate_fusion.15
  17.3 1.1 sqrt_multiply_fusion.15
  18.4 1.0 fusion.244
  20.2 0.8 convert_element_type.92
  21.1 0.9 convert_element_type.94
  22.0 0.9 fusion.58
  22.8 4.7 %all-to-all-start = ((f32[8,16,256]{2,1,0:T(8,128)}), f32[8,16,256]{2,1,0:T(8,128)S(1)}, u32[]{:S(2)}, u32[]{:S(2)}) async-start(f32[8,16,256]{2,1,0:T(8,128)} %bitcast.23), calls=%async_computation | async-start | bytes 262144 | tf_op jit(solution)/shard_map/all_to_all | solution.py:76
  27.7 1.1 sqrt_multiply_fusion.14
  28.8 3.0 %all-to-all-done = f32[8,16,256]{2,1,0:T(8,128)S(1)} async-done(((f32[8,16,256]{2,1,0:T(8,128)}), f32[8,16,256]{2,1,0:T(8,128)S(1)}, u32[]{:S(2)}, u32[]{:S(2)}) %all-to-all-start) | async-done | bytes 131104 | tf_op jit(solution)/shard_map/all_to_all | solution.py:76
  32.9 0.9 copy.81
  33.7 5.2 %all-to-all-start.1 = ((f32[8,2,16,256]{3,2,1,0:T(8,128)}), f32[8,2,16,256]{3,2,1,0:T(8,128)S(1)}, u32[]{:S(2)}, u32[]{:S(2)}) async-start(f32[8,2,16,256]{3,2,1,0:T(8,128)} %bitcast.25), calls=%async_computation.1 | async-start | bytes 524288 | tf_op jit(solution)/shard_map/all_to_all | solution.py:101
  39.1 0.8 copy.83
  39.9 4.4 %all-to-all-done.1 = f32[8,2,16,256]{3,2,1,0:T(8,128)S(1)} async-done(((f32[8,2,16,256]{3,2,1,0:T(8,128)}), f32[8,2,16,256]{3,2,1,0:T(8,128)S(1)}, u32[]{:S(2)}, u32[]{:S(2)}) %all-to-all-start.1) | async-done | bytes 262176 | tf_op jit(solution)/shard_map/all_to_all | solution.py:101
  44.3 5.2 %all-to-all-start.2 = ((f32[8,2,16,256]{3,2,1,0:T(8,128)}), f32[8,2,16,256]{3,2,1,0:T(8,128)S(1)}, u32[]{:S(2)}, u32[]{:S(2)}) async-start(f32[8,2,16,256]{3,2,1,0:T(8,128)} %bitcast.30), calls=%async_computation.2 | async-start | bytes 524288 | tf_op jit(solution)/shard_map/all_to_all | solution.py:108
  50.4 4.5 %all-to-all-done.2 = f32[8,2,16,256]{3,2,1,0:T(8,128)S(1)} async-done(((f32[8,2,16,256]{3,2,1,0:T(8,128)}), f32[8,2,16,256]{3,2,1,0:T(8,128)S(1)}, u32[]{:S(2)}, u32[]{:S(2)}) %all-to-all-start.2) | async-done | bytes 262176 | tf_op jit(solution)/shard_map/all_to_all | solution.py:108
  56.3 3.0 %multiply_subtract_fusion.1 = (f32[2,128,256]{1,2,0:T(8,128)S(1)}, f32[2,128,256]{1,2,0:T(8,128)S(1)}) fusion(f32[2,128,256]{1,2,0:T(8,128)S(1)} %fusion.2, f32[256]{0:T(256)S(1)} %bitcast.189, f32[256]{0:T(256)S(1)} %bitcast.265, f32[2,256]{1,0:T(2,128)S(1)} %get-tuple-element.113, f32[256]{0:T(256)S(1)} %bitcast.193, f32[256]{0:T(256)S(1)} %bitcast.191, ...), kind=kOutput, calls=%fused_computation.110 | convolution fusion | flops 113672192 | bytes 1378304 | tf_op jit(solution)/shard_map/bj,tjc->tbc/dot_general | solution.py:121
  59.3 2.5 %multiply_add_fusion.1 = f32[2,128,256]{1,2,0:T(8,128)S(1)} fusion(f32[2,128,256]{1,2,0:T(8,128)S(1)} %get-tuple-element.117, f32[2,128,256]{1,2,0:T(8,128)S(1)} %fusion.2, f32[256]{0:T(256)S(1)} %bitcast.190, f32[256]{0:T(256)S(1)} %bitcast.266, f32[2,256]{1,0:T(2,128)S(1)} %get-tuple-element.113, f32[256]{0:T(256)S(1)} %bitcast.194, f32[256]{0:T(256)S(1)} %bitcast.192, ...), kind=kLoop, calls=%fused_computation.109 | loop fusion | flops 12713984 | bytes 854016 | tf_op jit(solution)/shard_map/add | solution.py:130
  65.1 5.4 %all-to-all-start.3 = ((f32[2,8,16,256]{3,2,0,1:T(8,128)}), f32[2,8,16,256]{3,2,0,1:T(8,128)S(1)}, u32[]{:S(2)}, u32[]{:S(2)}) async-start(f32[2,8,16,256]{3,2,0,1:T(8,128)} %copy.64), calls=%async_computation.3 | async-start | bytes 524288 | tf_op jit(solution)/shard_map/all_to_all | solution.py:148
  71.2 4.7 %all-to-all-done.3 = f32[2,8,16,256]{3,2,0,1:T(8,128)S(1)} async-done(((f32[2,8,16,256]{3,2,0,1:T(8,128)}), f32[2,8,16,256]{3,2,0,1:T(8,128)S(1)}, u32[]{:S(2)}, u32[]{:S(2)}) %all-to-all-start.3) | async-done | bytes 262176 | tf_op jit(solution)/shard_map/all_to_all | solution.py:148
  75.9 5.1 %all-to-all-start.4 = ((f32[2,8,16,256]{3,2,0,1:T(8,128)}), f32[2,8,16,256]{3,2,0,1:T(8,128)S(1)}, u32[]{:S(2)}, u32[]{:S(2)}) async-start(f32[2,8,16,256]{3,2,0,1:T(8,128)} %copy.66), calls=%async_computation.4 | async-start | bytes 524288 | tf_op jit(solution)/shard_map/all_to_all | solution.py:155
  81.5 4.9 %all-to-all-done.4 = f32[2,8,16,256]{3,2,0,1:T(8,128)S(1)} async-done(((f32[2,8,16,256]{3,2,0,1:T(8,128)}), f32[2,8,16,256]{3,2,0,1:T(8,128)S(1)}, u32[]{:S(2)}, u32[]{:S(2)}) %all-to-all-start.4) | async-done | bytes 262176 | tf_op jit(solution)/shard_map/all_to_all | solution.py:155
  87.7 5.1 %all-to-all-start.5 = ((f32[2,8,16,256]{3,0,2,1:T(2,128)}), f32[2,8,16,256]{3,0,2,1:T(2,128)S(1)}, u32[]{:S(2)}, u32[]{:S(2)}) async-start(f32[2,8,16,256]{3,0,2,1:T(2,128)} %copy.68), calls=%async_computation.5 | async-start | bytes 524288 | tf_op jit(solution)/shard_map/all_to_all | solution.py:181
  92.7 3.1 %collective-permute-start = (bf16[6,256]{1,0:T(8,128)(2,1)S(1)}, bf16[6,256]{1,0:T(8,128)(2,1)S(1)}, u32[]{:S(2)}, u32[]{:S(2)}) collective-permute-start(bf16[6,256]{1,0:T(8,128)(2,1)S(1)} %slice.274), channel_id=1, source_target_pairs={{0,4},{4,8},{8,12},{12,16},{16,20},{20,24},{24,28},{1,5},{5,9},{9,... | collective-permute-start | bytes 9224 | tf_op jit(solution)/shard_map/ppermute | solution.py:12
  95.9 2.1 %collective-permute-done = bf16[6,256]{1,0:T(8,128)(2,1)S(1)} collective-permute-done((bf16[6,256]{1,0:T(8,128)(2,1)S(1)}, bf16[6,256]{1,0:T(8,128)(2,1)S(1)}, u32[]{:S(2)}, u32[]{:S(2)}) %collective-permute-start) | collective-permute-done | bytes 3104 | tf_op jit(solution)/shard_map/ppermute | solution.py:12
  98.3 1.0 fusion.92
  99.3 1.8 %fusion.246 = f32[128,4096]{1,0:T(8,128)} fusion(bf16[128,256]{1,0:T(8,128)(2,1)S(1)} %fusion.92, bf16[256,4096]{1,0:T(8,128)(2,1)S(1)} %copy-done), kind=kOutput, calls=%fused_computation.427 | convolution fusion | flops 268435456 | bytes 4259840 | tf_op jit(solution)/shard_map/dot_general | solution.py:198
  101.2 39.4 %reduce-scatter.2.cloned.1.call-done = f32[128,1024]{1,0:T(8,128)} async-done(((f32[128,4096]{1,0:T(8,128)}), f32[128,1024]{1,0:T(8,128)}) %reduce-scatter.2.cloned.1.call-update) | async-done | bytes 524304 | tf_op jit(solution)/shard_map/reduce_scatter | solution.py:199
  140.5 1.8 %convert_element_type.102 = bf16[128,1024]{1,0:T(8,128)(2,1)} convert(f32[128,1024]{1,0:T(8,128)} %reduce-scatter.2.cloned.1.call-done) | non-fusion elementwise | flops 131072 | bytes 786432 | tf_op jit(solution)/shard_map/convert_element_type | solution.py:199
  (46 shorter events, 12.2 us)
Async XLA Ops:
  6.5 92.8 %copy-start = (bf16[256,4096]{1,0:T(8,128)(2,1)S(1)}, bf16[256,4096]{1,0:T(8,128)(2,1)}, u32[]{:S(2)}) copy-start(bf16[256,4096]{1,0:T(8,128)(2,1)} %param.15) | copy-start | bytes 6291460
  7.4 14.5 %collective-permute-start.2 = (bf16[6,256]{1,0:T(8,128)(2,1)S(1)}, bf16[6,256]{1,0:T(8,128)(2,1)S(1)}, u32[]{:S(2)}, u32[]{:S(2)}) collective-permute-start(bf16[6,256]{1,0:T(8,128)(2,1)S(1)} %slice.302), channel_id=1, source_target_pairs={{0,4},{4,8},{8,12},{12,16},{16,20},{20,24},{24,28},{1,5},{5,9},{9,... | collective-permute-start | bytes 9224 | tf_op jit(solution)/shard_map/ppermute | solution.py:12
  11.2 10.7 %collective-permute-start.1 = (bf16[6,256]{1,0:T(8,128)(2,1)S(1)}, bf16[6,256]{1,0:T(8,128)(2,1)S(1)}, u32[]{:S(2)}, u32[]{:S(2)}) collective-permute-start(bf16[6,256]{1,0:T(8,128)(2,1)S(1)} %slice.288), channel_id=1, source_target_pairs={{0,4},{4,8},{8,12},{12,16},{16,20},{20,24},{24,28},{1,5},{5,9},{9,... | collective-permute-start | bytes 9224 | tf_op jit(solution)/shard_map/ppermute | solution.py:12
  22.8 9.0 %all-to-all-start = ((f32[8,16,256]{2,1,0:T(8,128)}), f32[8,16,256]{2,1,0:T(8,128)S(1)}, u32[]{:S(2)}, u32[]{:S(2)}) async-start(f32[8,16,256]{2,1,0:T(8,128)} %bitcast.23), calls=%async_computation | async-start | bytes 262144 | tf_op jit(solution)/shard_map/all_to_all | solution.py:76
  33.7 10.6 %all-to-all-start.1 = ((f32[8,2,16,256]{3,2,1,0:T(8,128)}), f32[8,2,16,256]{3,2,1,0:T(8,128)S(1)}, u32[]{:S(2)}, u32[]{:S(2)}) async-start(f32[8,2,16,256]{3,2,1,0:T(8,128)} %bitcast.25), calls=%async_computation.1 | async-start | bytes 524288 | tf_op jit(solution)/shard_map/all_to_all | solution.py:101
  44.3 10.5 %all-to-all-start.2 = ((f32[8,2,16,256]{3,2,1,0:T(8,128)}), f32[8,2,16,256]{3,2,1,0:T(8,128)S(1)}, u32[]{:S(2)}, u32[]{:S(2)}) async-start(f32[8,2,16,256]{3,2,1,0:T(8,128)} %bitcast.30), calls=%async_computation.2 | async-start | bytes 524288 | tf_op jit(solution)/shard_map/all_to_all | solution.py:108
  65.1 27.6 %copy-start.1 = (bf16[128,256]{1,0:T(8,128)(2,1)S(1)}, bf16[128,256]{1,0:T(8,128)(2,1)}, u32[]{:S(2)}) copy-start(bf16[128,256]{1,0:T(8,128)(2,1)} %param.8) | copy-start | bytes 196612
  65.1 10.8 %all-to-all-start.3 = ((f32[2,8,16,256]{3,2,0,1:T(8,128)}), f32[2,8,16,256]{3,2,0,1:T(8,128)S(1)}, u32[]{:S(2)}, u32[]{:S(2)}) async-start(f32[2,8,16,256]{3,2,0,1:T(8,128)} %copy.64), calls=%async_computation.3 | async-start | bytes 524288 | tf_op jit(solution)/shard_map/all_to_all | solution.py:148
  70.5 27.7 %copy-start.2 = (f32[256]{0:T(256)S(1)}, f32[256]{0:T(256)}, u32[]{:S(2)}) copy-start(f32[256]{0:T(256)} %param.14) | copy-start | bytes 3076
  75.9 10.4 %all-to-all-start.4 = ((f32[2,8,16,256]{3,2,0,1:T(8,128)}), f32[2,8,16,256]{3,2,0,1:T(8,128)S(1)}, u32[]{:S(2)}, u32[]{:S(2)}) async-start(f32[2,8,16,256]{3,2,0,1:T(8,128)} %copy.66), calls=%async_computation.4 | async-start | bytes 524288 | tf_op jit(solution)/shard_map/all_to_all | solution.py:155
  87.7 10.4 %all-to-all-start.5 = ((f32[2,8,16,256]{3,0,2,1:T(2,128)}), f32[2,8,16,256]{3,0,2,1:T(2,128)S(1)}, u32[]{:S(2)}, u32[]{:S(2)}) async-start(f32[2,8,16,256]{3,0,2,1:T(2,128)} %copy.68), calls=%async_computation.5 | async-start | bytes 524288 | tf_op jit(solution)/shard_map/all_to_all | solution.py:181
  92.7 47.8 %reduce-scatter.2.cloned.1.call-start = ((), (), s32[]{:S(2)}) async-start(), calls=%async_computation.7 | async-start | bytes 2621440 | tf_op jit(solution)/shard_map/reduce_scatter | solution.py:199
  92.7 5.3 %collective-permute-start = (bf16[6,256]{1,0:T(8,128)(2,1)S(1)}, bf16[6,256]{1,0:T(8,128)(2,1)S(1)}, u32[]{:S(2)}, u32[]{:S(2)}) collective-permute-start(bf16[6,256]{1,0:T(8,128)(2,1)S(1)} %slice.274), channel_id=1, source_target_pairs={{0,4},{4,8},{8,12},{12,16},{16,20},{20,24},{24,28},{1,5},{5,9},{9,... | collective-permute-start | bytes 9224 | tf_op jit(solution)/shard_map/ppermute | solution.py:12
Sparse Core Ops, SparseCore 0:
  101.3 39.2 reduce-scatter.1
where the time goes:
time: 152 us; the launch traced here: 149 us
  waiting for transfers between devices  63.1 us (42%)
  starting transfers between devices  40 us (26%)
  between operations  13.7 us (9%)
  other arithmetic  13.5 us (9%)
  matrix products  11.5 us (8%)
  local copies, waits for them, and re-layouts  7.48 us (5%)
    reduce_scatter x1, waiting for transfers between devices, local(): lax.psum_scatter(partial_out, 'tp', scatter_dimension=1, tiled=True)  39.4 us
    ppermute x3, starting transfers between devices, passed_along(): return lax.ppermute(block, axis, route)  9.37 us
    all_to_all x1, starting transfers between devices, local(): lax.all_to_all(w_real.reshape(2, shards, cols_dev, channels), 'seq', spli...  5.4 us
    all_to_all x1, starting transfers between devices, local(): lax.all_to_all(turned_real.reshape(shards, 2, cols_dev, channels), 'seq',...  5.21 us
    all_to_all x1, starting transfers between devices, local(): lax.all_to_all(turned_imag.reshape(shards, 2, cols_dev, channels), 'seq',...  5.17 us
    all_to_all x1, starting transfers between devices, local(): lax.all_to_all(w_imag.reshape(2, shards, cols_dev, channels), 'seq', spli...  5.06 us
    all_to_all x1, starting transfers between devices, local(): lax.all_to_all(out_real.reshape(2, shards, cols_dev, channels), 'seq', sp...  5.06 us
    all_to_all x1, waiting for transfers between devices, local(): lax.all_to_all(w_imag.reshape(2, shards, cols_dev, channels), 'seq', spli...  4.87 us
  transfers between devices with their start and end apart: 10, of which 8 were waited for; matrix products, arithmetic and copies ran while one was open for 8% of the time, Pallas kernels for 0%

commit v1 on v0

v1 whole, which is shorter than its diff:
```python
import functools

import jax
import jax.numpy as jnp
from jax import lax
from jax.experimental import pallas as pl
from jax.experimental.pallas import tpu as pltpu
from jax.sharding import PartitionSpec as P

MESH = pl.DeviceIdType.MESH
LANES = 128
SUB = 8
EDGE = 16
CHUNKS = 4


def one_minus_exp_neg(x):
    series = x * (1.0 - x * (1.0 / 2 - x * (1.0 / 6 - x * (1.0 / 24 - x * (1.0 / 120 - x * (1.0 / 720))))))
    return jnp.where(x < 0.2, series, 1.0 - jnp.exp(-x))


def kernel(
    n_seq,
    n_tp,
    query_hbm,
    key_hbm,
    value_hbm,
    taps_hbm,
    residue_hbm,
    rate_hbm,
    skip_hbm,
    weight_hbm,
    out_ref,
    streams,
    taps,
    residue,
    rate,
    skip,
    weight,
    halo,
    extended,
    gext,
    filt,
    conv,
    states,
    own_state,
    queries,
    hyena,
    far_send,
    far_recv,
    near_send,
    near_recv,
    cross_send,
    cross_recv,
    own_part,
    local_sem,
    halo_sem,
    state_send,
    state_recv,
    pair_send,
    pair_recv,
):
    rows, channels = query_hbm.shape
    order = rate_hbm.shape[0]
    n_taps = taps_hbm.shape[1]
    blocks = rows // SUB
    halves = channels // LANES
    width = out_ref.shape[1]
    piece = width // CHUNKS
    me = lax.axis_index("seq")
    tp = lax.axis_index("tp")
    twin = tp + 1 - 2 * lax.rem(tp, 2)
    cross = lax.rem(tp + 2, n_tp)
    twin_cross = lax.rem(twin + 2, n_tp)

    loads = [
        pltpu.make_async_copy(src, dst, local_sem.at[i])
        for i, (src, dst) in enumerate(
            (
                (key_hbm, streams.at[1]),
                (value_hbm, streams.at[2]),
                (query_hbm, streams.at[0]),
                (rate_hbm, rate),
                (residue_hbm, residue),
                (taps_hbm, taps),
                (skip_hbm, skip),
                (weight_hbm, weight),
            )
        )
    ]
    for load in loads:
        load.start()

    barrier = pltpu.get_barrier_semaphore()

    def greet(d, carry):
        pl.semaphore_signal(barrier, inc=1, device_id={"seq": d}, device_id_type=MESH)
        return carry

    lax.fori_loop(0, me, greet, 0)
    for partner in (twin, cross):
        pl.semaphore_signal(barrier, inc=1, device_id={"tp": partner}, device_id_type=MESH)
    for load in loads[:3]:
        load.wait()
    pl.semaphore_wait(barrier, n_seq - 1 - me + 2)

    def halo_copy(i):
        return pltpu.make_async_remote_copy(
            src_ref=streams.at[i, pl.ds(rows - EDGE, EDGE)],
            dst_ref=halo.at[i],
            send_sem=halo_sem.at[i],
            recv_sem=halo_sem.at[3 + i],
            device_id={"seq": lax.rem(me + 1, n_seq)},
            device_id_type=MESH,
        )

    @pl.when(me < n_seq - 1)
    def _():
        for i in (1, 2, 0):
            halo_copy(i).start()

    for load in loads[3:7]:
        load.wait()

    step = lax.broadcasted_iota(jnp.int32, (order, SUB, LANES), 1).astype(jnp.float32)

    def cube(x):
        return jnp.broadcast_to(x[:, None, :], (order, SUB, LANES))

    def amplitude_of(cols):
        return residue[:, cols] * jnp.sqrt(one_minus_exp_neg(2.0 * rate[:, cols]))

    for half in range(halves):
        cols = slice(half * LANES, (half + 1) * LANES)
        rates = cube(rate[:, cols])
        decay = jnp.exp(-float(SUB) * rates)
        term = cube(amplitude_of(cols)) * jnp.exp(-step * rates)
        for b in range(blocks):
            filt[b * SUB : (b + 1) * SUB, cols] = jnp.sum(term, axis=0)
            if b < blocks - 1:
                term = term * decay

    @pl.when(me == 0)
    def _():
        halo[...] = jnp.zeros_like(halo)

    @pl.when(me > 0)
    def _():
        for i in (1, 2, 0):
            halo_copy(i).wait_recv()

    def short_conv(i):
        extended[i, 0:SUB] = halo[i].astype(jnp.float32)[EDGE - SUB :]
        extended[i, SUB:] = streams[i].astype(jnp.float32)
        total = jnp.zeros((rows, channels), jnp.float32)
        for t in range(n_taps):
            total = total + taps[i, t : t + 1, :] * extended[i, SUB - t : SUB - t + rows]
        return total

    gext[0:SUB] = jnp.zeros((SUB, channels), jnp.float32)
    gext[SUB:] = short_conv(1) * short_conv(2)

    for half in range(halves):
        cols = slice(half * LANES, (half + 1) * LANES)
        rates = cube(rate[:, cols])
        decay = jnp.exp(-float(SUB) * rates)
        total = jnp.broadcast_to(gext[SUB : 2 * SUB, cols][None], (order, SUB, LANES))
        for b in range(1, blocks):
            total = total * decay + gext[(b + 1) * SUB : (b + 2) * SUB, cols][None]
        total = total * jnp.exp((step - float(SUB - 1)) * rates)
        own_state[:, cols] = jnp.sum(total, axis=1)

    def state_copy(slot, d):
        return pltpu.make_async_remote_copy(
            src_ref=own_state,
            dst_ref=states.at[slot],
            send_sem=state_send.at[d],
            recv_sem=state_recv.at[slot],
            device_id={"seq": d},
            device_id_type=MESH,
        )

    def send_state(d, carry):
        state_copy(me, d).start()
        return carry

    lax.fori_loop(me + 1, n_seq, send_state, 0)

    queries[...] = short_conv(0)

    def local_conv(half, carry):
        cols = pl.ds(pl.multiple_of(half * LANES, LANES), LANES)
        total = jnp.zeros((rows, LANES), jnp.float32)
        for s in range(SUB):
            shifted = gext[SUB - s : SUB - s + rows, cols]
            for q in range(blocks):
                tap = filt[q * SUB + s : q * SUB + s + 1, cols]
                if q == 0:
                    total = total + tap * shifted
                else:
                    lower = total[q * SUB :] + tap * shifted[: rows - q * SUB]
                    total = jnp.concatenate([total[: q * SUB], lower], axis=0)
        conv[:, cols] = total
        return carry

    lax.fori_loop(0, halves, local_conv, 0)

    span = jnp.exp(-float(rows) * rate[...])

    def take_state(d, held):
        state_copy(d, d).wait_recv()
        return held * span + states[d]

    held = lax.fori_loop(0, me, take_state, jnp.zeros((order, channels), jnp.float32))

    for half in range(halves):
        cols = slice(half * LANES, (half + 1) * LANES)
        rates = cube(rate[:, cols])
        decay = jnp.exp(-float(SUB) * rates)
        term = cube(amplitude_of(cols) * held[:, cols]) * jnp.exp(-(step + 1.0) * rates)
        direct = skip[:, cols]
        for b in range(blocks):
            here = slice(b * SUB, (b + 1) * SUB)
            gated = gext[(b + 1) * SUB : (b + 2) * SUB, cols]
            total = conv[here, cols] + jnp.sum(term, axis=0)
            queries[here, cols] = queries[here, cols] * (total + direct * gated)
            if b < blocks - 1:
                term = term * decay
    hyena[...] = queries[...].astype(jnp.bfloat16)

    loads[7].wait()

    def product(block, c):
        cols = pl.ds(pl.multiple_of(block * width + c * piece, piece), piece)
        return jnp.dot(hyena[...], weight[:, cols], preferred_element_type=jnp.float32)

    def pair_copy(kind, c):
        src, dst, target = (
            (far_send, far_recv, twin),
            (cross_send, cross_recv, cross),
            (near_send, near_recv, twin),
        )[kind]
        return pltpu.make_async_remote_copy(
            src_ref=src.at[c],
            dst_ref=dst.at[c],
            send_sem=pair_send.at[kind * CHUNKS + c],
            recv_sem=pair_recv.at[kind * CHUNKS + c],
            device_id={"tp": target},
            device_id_type=MESH,
        )

    for c in range(CHUNKS):
        far_send[c] = product(twin_cross, c).astype(jnp.bfloat16)
        pair_copy(0, c).start()
    for c in range(CHUNKS):
        mine = product(cross, c)
        pair_copy(0, c).wait_recv()
        cross_send[c] = (mine + far_recv[c].astype(jnp.float32)).astype(jnp.bfloat16)
        pair_copy(1, c).start()
    for c in range(CHUNKS):
        near_send[c] = product(twin, c).astype(jnp.bfloat16)
        pair_copy(2, c).start()
    for c in range(CHUNKS):
        own_part[c] = product(tp, c)
    for c in range(CHUNKS):
        pair_copy(2, c).wait_recv()
        own_part[c] = own_part[c] + near_recv[c].astype(jnp.float32)
    for c in range(CHUNKS):
        pair_copy(1, c).wait_recv()
        total = own_part[c] + cross_recv[c].astype(jnp.float32)
        out_ref[:, c * piece : (c + 1) * piece] = total.astype(out_ref.dtype)

    for kind in range(3):
        for c in range(CHUNKS):
            pair_copy(kind, c).wait_send()

    @pl.when(me < n_seq - 1)
    def _():
        for i in (1, 2, 0):
            halo_copy(i).wait_send()

    def sent_state(d, carry):
        state_copy(me, d).wait_send()
        return carry

    lax.fori_loop(me + 1, n_seq, sent_state, 0)


def solution(mesh):
    n_seq, n_tp = mesh.shape["seq"], mesh.shape["tp"]
    assert n_tp == 4

    def local(query_in, key_in, value_in, short_weight, residue, rate, skip, out_weight):
        rows, channels = query_in.shape
        order, n_taps = rate.shape[0], short_weight.shape[1]
        total_width = out_weight.shape[1]
        width = total_width // n_tp
        piece = width // CHUNKS
        f32, bf16 = jnp.float32, jnp.bfloat16
        pieces = pltpu.VMEM((CHUNKS, rows, piece), bf16)
        return pl.pallas_call(
            functools.partial(kernel, n_seq, n_tp),
            out_shape=jax.ShapeDtypeStruct((rows, width), bf16),
            in_specs=[pl.BlockSpec(memory_space=pl.ANY)] * 8,
            out_specs=pl.BlockSpec(memory_space=pltpu.VMEM),
            scratch_shapes=[
                pltpu.VMEM((3, rows, channels), bf16),
                pltpu.VMEM((3, n_taps, channels), f32),
                pltpu.VMEM((order, channels), f32),
                pltpu.VMEM((order, channels), f32),
                pltpu.VMEM((1, channels), f32),
                pltpu.VMEM((channels, total_width), bf16),
                pltpu.VMEM((3, EDGE, channels), bf16),
                pltpu.VMEM((3, rows + SUB, channels), f32),
                pltpu.VMEM((rows + SUB, channels), f32),
                pltpu.VMEM((rows, channels), f32),
                pltpu.VMEM((rows, channels), f32),
                pltpu.VMEM((n_seq, order, channels), f32),
                pltpu.VMEM((order, channels), f32),
                pltpu.VMEM((rows, channels), f32),
                pltpu.VMEM((rows, channels), bf16),
                pieces,
                pieces,
                pieces,
                pieces,
                pieces,
                pieces,
                pltpu.VMEM((CHUNKS, rows, piece), f32),
                pltpu.SemaphoreType.DMA((8,)),
                pltpu.SemaphoreType.DMA((6,)),
                pltpu.SemaphoreType.DMA((n_seq,)),
                pltpu.SemaphoreType.DMA((n_seq,)),
                pltpu.SemaphoreType.DMA((3 * CHUNKS,)),
                pltpu.SemaphoreType.DMA((3 * CHUNKS,)),
            ],
            compiler_params=pltpu.CompilerParams(
                collective_id=0, has_side_effects=True, vmem_limit_bytes=40 * 1024 * 1024
            ),
        )(
            query_in,
            key_in,
            value_in,
            short_weight,
            residue,
            rate,
            skip.reshape(1, channels),
            out_weight,
        )

    in_specs = (
        P("seq", "tp"),
        P("seq", "tp"),
        P("seq", "tp"),
        P(None, None, "tp"),
        P(None, "tp"),
        P(None, "tp"),
        P("tp"),
        P("tp", None),
    )
    return jax.shard_map(local, mesh=mesh, in_specs=in_specs, out_specs=P("seq", "tp"), check_vma=False)
```

time: 152 us -> 30.1 us (0.20)
  the two profiles are of different devices: /device:TPU:9 before, /device:TPU:25 now
where the time goes in v1:
time: 30.1 us; the launch traced here: 29.7 us
  Pallas kernels  22 us (73%)
  local copies, waits for them, and re-layouts  7.66 us (25%)
    pallas_call x1, Pallas kernels, local(): pl.pallas_call(functools.partial(kernel, n_seq, n_tp), out_shape=jax.Shap...  22 us
    unnamed x17, local copies, waits for them, and re-layouts  7.66 us

profile of v1, /device:TPU:25, one launch (start us, length us, event | category | flops | bytes accessed | tf_op | source)
XLA Modules:
  0.0 29.7 jit_solution(17346337551408708424)
XLA Ops:
  0.0 0.0 copy-start
  0.0 1.6 %copy-done = bf16[256,4096]{1,0:T(8,128)(2,1)S(1)} copy-done((bf16[256,4096]{1,0:T(8,128)(2,1)S(1)}, bf16[256,4096]{1,0:T(8,128)(2,1)}, u32[]{:S(2)}) %copy-start) | copy-done | bytes 2097176
  1.6 0.0 copy-start.1
  1.6 0.8 %copy-done.1 = bf16[128,256]{1,0:T(8,128)(2,1)S(1)} copy-done((bf16[128,256]{1,0:T(8,128)(2,1)S(1)}, bf16[128,256]{1,0:T(8,128)(2,1)}, u32[]{:S(2)}) %copy-start.1) | copy-done | bytes 65560
  2.4 0.0 copy-start.2
  2.4 0.8 %copy-done.2 = bf16[128,256]{1,0:T(8,128)(2,1)S(1)} copy-done((bf16[128,256]{1,0:T(8,128)(2,1)S(1)}, bf16[128,256]{1,0:T(8,128)(2,1)}, u32[]{:S(2)}) %copy-start.2) | copy-done | bytes 65560
  3.3 0.0 copy-start.3
  3.3 0.8 %copy-done.3 = bf16[128,256]{1,0:T(8,128)(2,1)S(1)} copy-done((bf16[128,256]{1,0:T(8,128)(2,1)S(1)}, bf16[128,256]{1,0:T(8,128)(2,1)}, u32[]{:S(2)}) %copy-start.3) | copy-done | bytes 65560
  4.1 0.0 copy-start.4
  4.1 0.7 %copy-done.4 = f32[3,7,256]{2,1,0:T(8,128)S(1)} copy-done((f32[3,7,256]{2,1,0:T(8,128)S(1)}, f32[3,7,256]{2,1,0:T(8,128)}, u32[]{:S(2)}) %copy-start.4) | copy-done | bytes 21528
  4.8 0.0 copy-start.5
  4.9 0.7 %copy-done.5 = f32[16,256]{1,0:T(8,128)S(1)} copy-done((f32[16,256]{1,0:T(8,128)S(1)}, f32[16,256]{1,0:T(8,128)}, u32[]{:S(2)}) %copy-start.5) | copy-done | bytes 16408
  5.6 0.0 copy-start.6
  5.6 0.7 %copy-done.6 = f32[16,256]{1,0:T(8,128)S(1)} copy-done((f32[16,256]{1,0:T(8,128)S(1)}, f32[16,256]{1,0:T(8,128)}, u32[]{:S(2)}) %copy-start.6) | copy-done | bytes 16408
  6.3 0.0 copy-start.7
  6.3 0.7 %copy-done.7 = f32[256]{0:T(256)S(1)} copy-done((f32[256]{0:T(256)S(1)}, f32[256]{0:T(256)}, u32[]{:S(2)}) %copy-start.7) | copy-done | bytes 1048
  7.0 22.0 %shard_map.82 = bf16[128,1024]{1,0:T(8,128)(2,1)S(1)} custom-call(bf16[128,256]{1,0:T(8,128)(2,1)S(1)} %copy-done.1, bf16[128,256]{1,0:T(8,128)(2,1)S(1)} %copy-done.2, bf16[128,256]{1,0:T(8,128)(2,1)S(1)} %copy-done.3, f32[3,7,256]{2,1,0:T(8,128)S(1)} %copy-done.4, f32[16,256]{1,0:T(8,128)S(1)} %copy-done.5, f32[16,256]{1,0:T(8,128)S(1)} %copy-done.6, ...), custom_call_target="tpu_custom_call" | custom-call | tf_op jit(solution)/shard_map/pallas_call | solution.py:301
  29.0 0.7 %copy.10 = bf16[128,1024]{1,0:T(8,128)(2,1)} copy(bf16[128,1024]{1,0:T(8,128)(2,1)S(1)} %shard_map.82) | data formatting | bytes 524288
Async XLA Ops:
  0.0 1.6 %copy-start = (bf16[256,4096]{1,0:T(8,128)(2,1)S(1)}, bf16[256,4096]{1,0:T(8,128)(2,1)}, u32[]{:S(2)}) copy-start(bf16[256,4096]{1,0:T(8,128)(2,1)} %weight_hbm.1) | copy-start | bytes 6291460
  1.6 0.8 %copy-start.1 = (bf16[128,256]{1,0:T(8,128)(2,1)S(1)}, bf16[128,256]{1,0:T(8,128)(2,1)}, u32[]{:S(2)}) copy-start(bf16[128,256]{1,0:T(8,128)(2,1)} %query_hbm.1) | copy-start | bytes 196612
  2.4 0.8 %copy-start.2 = (bf16[128,256]{1,0:T(8,128)(2,1)S(1)}, bf16[128,256]{1,0:T(8,128)(2,1)}, u32[]{:S(2)}) copy-start(bf16[128,256]{1,0:T(8,128)(2,1)} %key_hbm.1) | copy-start | bytes 196612
  3.3 0.8 %copy-start.3 = (bf16[128,256]{1,0:T(8,128)(2,1)S(1)}, bf16[128,256]{1,0:T(8,128)(2,1)}, u32[]{:S(2)}) copy-start(bf16[128,256]{1,0:T(8,128)(2,1)} %value_hbm.1) | copy-start | bytes 196612
  4.1 0.7 %copy-start.4 = (f32[3,7,256]{2,1,0:T(8,128)S(1)}, f32[3,7,256]{2,1,0:T(8,128)}, u32[]{:S(2)}) copy-start(f32[3,7,256]{2,1,0:T(8,128)} %taps_hbm.1) | copy-start | bytes 64516
  4.8 0.7 %copy-start.5 = (f32[16,256]{1,0:T(8,128)S(1)}, f32[16,256]{1,0:T(8,128)}, u32[]{:S(2)}) copy-start(f32[16,256]{1,0:T(8,128)} %residue_hbm.1) | copy-start | bytes 49156
  5.6 0.7 %copy-start.6 = (f32[16,256]{1,0:T(8,128)S(1)}, f32[16,256]{1,0:T(8,128)}, u32[]{:S(2)}) copy-start(f32[16,256]{1,0:T(8,128)} %rate_hbm.1) | copy-start | bytes 49156
  6.3 0.7 %copy-start.7 = (f32[256]{0:T(256)S(1)}, f32[256]{0:T(256)}, u32[]{:S(2)}) copy-start(f32[256]{0:T(256)} %param.14) | copy-start | bytes 3076

commit v2 on v1

v2 whole, which is shorter than its diff:
```python
import functools

import jax
import jax.numpy as jnp
from jax import lax
from jax.experimental import pallas as pl
from jax.experimental.pallas import tpu as pltpu
from jax.sharding import PartitionSpec as P

MESH = pl.DeviceIdType.MESH
LANES = 128
SUB = 8
EDGE = 16
CHUNKS = 4


def one_minus_exp_neg(x):
    series = x * (1.0 - x * (1.0 / 2 - x * (1.0 / 6 - x * (1.0 / 24 - x * (1.0 / 120 - x * (1.0 / 720))))))
    return jnp.where(x < 0.2, series, 1.0 - jnp.exp(-x))


def kernel(
    n_seq,
    n_tp,
    query_hbm,
    key_hbm,
    value_hbm,
    taps_hbm,
    residue_hbm,
    rate_hbm,
    skip_hbm,
    weight_hbm,
    out_ref,
    streams,
    taps,
    residue,
    rate,
    skip,
    weight,
    halo,
    extended,
    gext,
    fext,
    conv,
    states,
    own_state,
    heads,
    own_head,
    queries,
    hyena,
    twin_hyena,
    cross_send,
    cross_recv,
    own_part,
    local_sem,
    halo_sem,
    state_send,
    state_recv,
    head_send,
    head_recv,
    twin_sem,
    cross_out,
    cross_in,
):
    rows, channels = query_hbm.shape
    order = rate_hbm.shape[0]
    n_taps = taps_hbm.shape[1]
    blocks = rows // SUB
    halves = channels // LANES
    width = out_ref.shape[1]
    piece = width // CHUNKS
    me = lax.axis_index("seq")
    tp = lax.axis_index("tp")
    twin = tp + 1 - 2 * lax.rem(tp, 2)
    cross = lax.rem(tp + 2, n_tp)
    twin_cross = lax.rem(twin + 2, n_tp)

    def columns(block):
        return pl.ds(pl.multiple_of(block * width, width), width)

    own_rows, twin_rows = pl.ds(0, channels), pl.ds(channels, channels)
    loads = [
        pltpu.make_async_copy(src, dst, local_sem.at[i])
        for i, (src, dst) in enumerate(
            (
                (rate_hbm, rate),
                (residue_hbm, residue),
                (key_hbm, streams.at[1]),
                (value_hbm, streams.at[2]),
                (taps_hbm, taps),
                (query_hbm, streams.at[0]),
                (skip_hbm, skip),
                (weight_hbm.at[:, columns(cross)], weight.at[0, own_rows]),
                (weight_hbm.at[:, columns(tp)], weight.at[1, own_rows]),
            )
        )
    ]
    for load in loads:
        load.start()

    barrier = pltpu.get_barrier_semaphore()

    def greet(d, carry):
        pl.semaphore_signal(barrier, inc=1, device_id={"seq": d}, device_id_type=MESH)
        return carry

    lax.fori_loop(0, me, greet, 0)
    for partner in (twin, cross):
        pl.semaphore_signal(barrier, inc=1, device_id={"tp": partner}, device_id_type=MESH)

    step = lax.broadcasted_iota(jnp.int32, (order, SUB, LANES), 1).astype(jnp.float32)
    lanes = [slice(half * LANES, (half + 1) * LANES) for half in range(halves)]

    def cube(x):
        return jnp.broadcast_to(x[:, None, :], (order, SUB, LANES))

    def amplitude_of(cols):
        return residue[:, cols] * jnp.sqrt(one_minus_exp_neg(2.0 * rate[:, cols]))

    for load in loads[:2]:
        load.wait()
    fext[0:SUB] = jnp.zeros((SUB, channels), jnp.float32)
    for cols in lanes:
        rates = cube(rate[:, cols])
        decay = jnp.exp(-float(SUB) * rates)
        term = cube(amplitude_of(cols)) * jnp.exp(-step * rates)
        for b in range(blocks):
            fext[(b + 1) * SUB : (b + 2) * SUB, cols] = jnp.sum(term, axis=0)
            if b < blocks - 1:
                term = term * decay

    for load in loads[2:6]:
        load.wait()

    def short_conv(i, first, count):
        total = jnp.zeros((count, channels), jnp.float32)
        for t in range(n_taps):
            begin = first + SUB - t
            total = total + taps[i, t : t + 1, :] * extended[i, begin : begin + count]
        return total

    for i in range(3):
        extended[i, SUB:] = streams[i].astype(jnp.float32)
    gext[0 : 2 * SUB] = jnp.zeros((2 * SUB, channels), jnp.float32)
    gext[2 * SUB :] = short_conv(1, SUB, rows - SUB) * short_conv(2, SUB, rows - SUB)

    for cols in lanes:
        rates = cube(rate[:, cols])
        decay = jnp.exp(-float(SUB) * rates)
        total = jnp.broadcast_to(gext[2 * SUB : 3 * SUB, cols][None], (order, SUB, LANES))
        for b in range(2, blocks):
            total = total * decay + gext[(b + 1) * SUB : (b + 2) * SUB, cols][None]
        total = total * jnp.exp((step - float(SUB - 1)) * rates)
        own_state[:, cols] = jnp.sum(total, axis=1)

    pl.semaphore_wait(barrier, n_seq - 1 - me + 2)

    def halo_copy(i):
        return pltpu.make_async_remote_copy(
            src_ref=streams.at[i, pl.ds(rows - EDGE, EDGE)],
            dst_ref=halo.at[i],
            send_sem=halo_sem.at[i],
            recv_sem=halo_sem.at[3 + i],
            device_id={"seq": lax.rem(me + 1, n_seq)},
            device_id_type=MESH,
        )

    def state_copy(slot, d):
        return pltpu.make_async_remote_copy(
            src_ref=own_state,
            dst_ref=states.at[slot],
            send_sem=state_send.at[d],
            recv_sem=state_recv.at[slot],
            device_id={"seq": d},
            device_id_type=MESH,
        )

    def head_copy(slot, d):
        return pltpu.make_async_remote_copy(
            src_ref=own_head,
            dst_ref=heads.at[slot],
            send_sem=head_send.at[d],
            recv_sem=head_recv.at[slot],
            device_id={"seq": d},
            device_id_type=MESH,
        )

    def weight_copy(i):
        return pltpu.make_async_remote_copy(
            src_ref=weight_hbm.at[:, columns((twin_cross, twin)[i])],
            dst_ref=weight.at[i, twin_rows],
            send_sem=twin_sem.at[i],
            recv_sem=twin_sem.at[3 + i],
            device_id={"tp": twin},
            device_id_type=MESH,
        )

    hyena_copy = pltpu.make_async_remote_copy(
        src_ref=hyena,
        dst_ref=twin_hyena,
        send_sem=twin_sem.at[2],
        recv_sem=twin_sem.at[5],
        device_id={"tp": twin},
        device_id_type=MESH,
    )

    def cross_copy(c):
        return pltpu.make_async_remote_copy(
            src_ref=cross_send.at[c],
            dst_ref=cross_recv.at[c],
            send_sem=cross_out.at[c],
            recv_sem=cross_in.at[c],
            device_id={"tp": cross},
            device_id_type=MESH,
        )

    @pl.when(me < n_seq - 1)
    def _():
        for i in (1, 2, 0):
            halo_copy(i).start()

    def send_state(d, carry):
        state_copy(me, d).start()
        return carry

    lax.fori_loop(me + 1, n_seq, send_state, 0)
    for i in range(2):
        weight_copy(i).start()

    def local_conv(half, carry):
        cols = pl.ds(pl.multiple_of(half * LANES, LANES), LANES)
        total = jnp.zeros((rows, LANES), jnp.float32)
        for s in range(SUB):
            shifted = gext[SUB - s : SUB - s + rows, cols]
            for q in range(blocks):
                tap = fext[(q + 1) * SUB + s : (q + 1) * SUB + s + 1, cols]
                if q == 0:
                    total = total + tap * shifted
                else:
                    lower = total[q * SUB :] + tap * shifted[: rows - q * SUB]
                    total = jnp.concatenate([total[: q * SUB], lower], axis=0)
        conv[:, cols] = total
        return carry

    lax.fori_loop(0, halves, local_conv, 0)

    @pl.when(me == 0)
    def _():
        halo[...] = jnp.zeros_like(halo)

    @pl.when(me > 0)
    def _():
        for i in (1, 2, 0):
            halo_copy(i).wait_recv()

    for i in range(3):
        extended[i, 0:SUB] = halo[i].astype(jnp.float32)[EDGE - SUB :]
    head = short_conv(1, 0, SUB) * short_conv(2, 0, SUB)
    own_head[...] = head
    gext[SUB : 2 * SUB] = head

    def send_head(d, carry):
        head_copy(me, d).start()
        return carry

    lax.fori_loop(me + 1, n_seq, send_head, 0)

    queries[...] = short_conv(0, 0, rows)
    for cols in lanes:
        total = conv[:, cols]
        for j in range(SUB):
            total = total + own_head[j : j + 1, cols] * fext[SUB - j : SUB - j + rows, cols]
        conv[:, cols] = total

    loads[6].wait()
    spans = jnp.exp(-float(rows) * rate[...])
    wide = jnp.broadcast_to(spans[:, None, :], (order, SUB, channels))

    def take_state(d, carry):
        held, front = carry
        state_copy(d, d).wait_recv()
        head_copy(d, d).wait_recv()
        return held * spans + states[d], front * wide + heads[d][None]

    held, front = lax.fori_loop(
        0,
        me,
        take_state,
        (
            jnp.zeros((order, channels), jnp.float32),
            jnp.zeros((order, SUB, channels), jnp.float32),
        ),
    )

    for cols in lanes:
        rates = cube(rate[:, cols])
        decay = jnp.exp(-float(SUB) * rates)
        ahead = jnp.exp((step - float(rows - 1)) * rates) * front[:, :, cols]
        carried = amplitude_of(cols) * (held[:, cols] + jnp.sum(ahead, axis=1))
        term = cube(carried) * jnp.exp(-(step + 1.0) * rates)
        direct = skip[:, cols]
        for b in range(blocks):
            here = slice(b * SUB, (b + 1) * SUB)
            gated = gext[(b + 1) * SUB : (b + 2) * SUB, cols]
            total = conv[here, cols] + jnp.sum(term, axis=0)
            queries[here, cols] = queries[here, cols] * (total + direct * gated)
            if b < blocks - 1:
                term = term * decay
    hyena[...] = queries[...].astype(jnp.bfloat16)
    hyena_copy.start()

    def product(rows_of, block, c, part):
        tile = weight[block, part * channels : (part + 1) * channels, c * piece : (c + 1) * piece]
        return jnp.dot(rows_of[...], tile, preferred_element_type=jnp.float32)

    loads[7].wait()
    for c in range(CHUNKS):
        own_part[c] = product(hyena, 0, c, 0)
    weight_copy(0).wait_recv()
    hyena_copy.wait_recv()
    for c in range(CHUNKS):
        cross_send[c] = (own_part[c] + product(twin_hyena, 0, c, 1)).astype(jnp.bfloat16)
        cross_copy(c).start()
    loads[8].wait()
    weight_copy(1).wait_recv()
    for c in range(CHUNKS):
        own_part[c] = product(hyena, 1, c, 0) + product(twin_hyena, 1, c, 1)
    for c in range(CHUNKS):
        cross_copy(c).wait_recv()
        total = own_part[c] + cross_recv[c].astype(jnp.float32)
        out_ref[:, c * piece : (c + 1) * piece] = total.astype(out_ref.dtype)

    for c in range(CHUNKS):
        cross_copy(c).wait_send()
    for i in range(2):
        weight_copy(i).wait_send()
    hyena_copy.wait_send()

    @pl.when(me < n_seq - 1)
    def _():
        for i in (1, 2, 0):
            halo_copy(i).wait_send()

    def sent(d, carry):
        state_copy(me, d).wait_send()
        head_copy(me, d).wait_send()
        return carry

    lax.fori_loop(me + 1, n_seq, sent, 0)


def solution(mesh):
    n_seq, n_tp = mesh.shape["seq"], mesh.shape["tp"]
    assert n_tp == 4

    def local(query_in, key_in, value_in, short_weight, residue, rate, skip, out_weight):
        rows, channels = query_in.shape
        order, n_taps = rate.shape[0], short_weight.shape[1]
        width = out_weight.shape[1] // n_tp
        piece = width // CHUNKS
        f32, bf16 = jnp.float32, jnp.bfloat16
        pieces = pltpu.VMEM((CHUNKS, rows, piece), bf16)
        return pl.pallas_call(
            functools.partial(kernel, n_seq, n_tp),
            out_shape=jax.ShapeDtypeStruct((rows, width), bf16),
            in_specs=[pl.BlockSpec(memory_space=pltpu.HBM)] * 8,
            out_specs=pl.BlockSpec(memory_space=pltpu.VMEM),
            scratch_shapes=[
                pltpu.VMEM((3, rows, channels), bf16),
                pltpu.VMEM((3, n_taps, channels), f32),
                pltpu.VMEM((order, channels), f32),
                pltpu.VMEM((order, channels), f32),
                pltpu.VMEM((1, channels), f32),
                pltpu.VMEM((2, 2 * channels, width), bf16),
                pltpu.VMEM((3, EDGE, channels), bf16),
                pltpu.VMEM((3, rows + SUB, channels), f32),
                pltpu.VMEM((rows + SUB, channels), f32),
                pltpu.VMEM((rows + SUB, channels), f32),
                pltpu.VMEM((rows, channels), f32),
                pltpu.VMEM((n_seq, order, channels), f32),
                pltpu.VMEM((order, channels), f32),
                pltpu.VMEM((n_seq, SUB, channels), f32),
                pltpu.VMEM((SUB, channels), f32),
                pltpu.VMEM((rows, channels), f32),
                pltpu.VMEM((rows, channels), bf16),
                pltpu.VMEM((rows, channels), bf16),
                pieces,
                pieces,
                pltpu.VMEM((CHUNKS, rows, piece), f32),
                pltpu.SemaphoreType.DMA((9,)),
                pltpu.SemaphoreType.DMA((6,)),
                pltpu.SemaphoreType.DMA((n_seq,)),
                pltpu.SemaphoreType.DMA((n_seq,)),
                pltpu.SemaphoreType.DMA((n_seq,)),
                pltpu.SemaphoreType.DMA((n_seq,)),
                pltpu.SemaphoreType.DMA((6,)),
                pltpu.SemaphoreType.DMA((CHUNKS,)),
                pltpu.SemaphoreType.DMA((CHUNKS,)),
            ],
            compiler_params=pltpu.CompilerParams(
                collective_id=0, has_side_effects=True, vmem_limit_bytes=60 * 1024 * 1024
            ),
        )(
            query_in,
            key_in,
            value_in,
            short_weight,
            residue,
            rate,
            skip.reshape(1, channels),
            out_weight,
        )

    in_specs = (
        P("seq", "tp"),
        P("seq", "tp"),
        P("seq", "tp"),
        P(None, None, "tp"),
        P(None, "tp"),
        P(None, "tp"),
        P("tp"),
        P("tp", None),
    )
    return jax.shard_map(local, mesh=mesh, in_specs=in_specs, out_specs=P("seq", "tp"), check_vma=False)
```

time: 30.1 us -> 22.7 us (0.75)
  the two profiles are of different devices: /device:TPU:25 before, /device:TPU:9 now
where the time goes in v2:
time: 22.7 us; the launch traced here: 22.2 us
  Pallas kernels  20.5 us (90%)
  local copies, waits for them, and re-layouts  1.67 us (7%)
    pallas_call x1, Pallas kernels, local(): pl.pallas_call(functools.partial(kernel, n_seq, n_tp), out_shape=jax.Shap...  20.5 us
    unnamed x1, local copies, waits for them, and re-layouts  1.67 us

profile of v2, /device:TPU:9, one launch (start us, length us, event | category | flops | bytes accessed | tf_op | source)
XLA Modules:
  0.0 22.2 jit_solution(12316573529595760069)
XLA Ops:
  0.0 20.5 %shard_map.82 = bf16[128,1024]{1,0:T(8,128)(2,1)} custom-call(bf16[128,256]{1,0:T(8,128)(2,1)} %query_hbm.1, bf16[128,256]{1,0:T(8,128)(2,1)} %key_hbm.1, bf16[128,256]{1,0:T(8,128)(2,1)} %value_hbm.1, f32[3,7,256]{2,1,0:T(8,128)} %taps_hbm.1, f32[16,256]{1,0:T(8,128)} %residue_hbm.1, f32[16,256]{1,0:T(8,128)} %rate_hbm.1, f32[1,256]{1,0:T(1,128)} %bitcast.1, ...), custom_call_target="tpu_custom_call" | custom-call | tf_op jit(solution)/shard_map/pallas_call | solution.py:363
  20.6 1.7 %copy.10 = bf16[128,1024]{1,0:T(8,128)(2,1)} copy(bf16[128,1024]{1,0:T(8,128)(2,1)} %shard_map.82) | data formatting | bytes 524288

commit v3 on v2

--- a/solution.py
+++ b/solution.py
@@ -12,6 +12,7 @@
 SUB = 8
 EDGE = 16
 CHUNKS = 4
+EARLY = 2
 
 
 def one_minus_exp_neg(x):
@@ -30,13 +31,15 @@
     rate_hbm,
     skip_hbm,
     weight_hbm,
-    out_ref,
+    out_hbm,
     streams,
     taps,
     residue,
     rate,
     skip,
     weight,
+    cross_weight,
+    far_weight,
     halo,
     extended,
     gext,
@@ -49,6 +52,9 @@
     queries,
     hyena,
     twin_hyena,
+    cross_hyena,
+    far_hyena,
+    result,
     cross_send,
     cross_recv,
     own_part,
@@ -58,16 +64,18 @@
     state_recv,
     head_send,
     head_recv,
-    twin_sem,
+    tp_out,
+    tp_in,
     cross_out,
     cross_in,
+    result_sem,
 ):
     rows, channels = query_hbm.shape
     order = rate_hbm.shape[0]
     n_taps = taps_hbm.shape[1]
     blocks = rows // SUB
     halves = channels // LANES
-    width = out_ref.shape[1]
+    width = out_hbm.shape[1]
     piece = width // CHUNKS
     me = lax.axis_index("seq")
     tp = lax.axis_index("tp")
@@ -75,8 +83,10 @@
     cross = lax.rem(tp + 2, n_tp)
     twin_cross = lax.rem(twin + 2, n_tp)
 
-    def columns(block):
-        return pl.ds(pl.multiple_of(block * width, width), width)
+    early = EARLY * piece
+
+    def columns(block, first=0, count=width):
+        return pl.ds(pl.multiple_of(block * width + first, piece), count)
 
     own_rows, twin_rows = pl.ds(0, channels), pl.ds(channels, channels)
     loads = [
@@ -90,8 +100,8 @@
                 (taps_hbm, taps),
                 (query_hbm, streams.at[0]),
                 (skip_hbm, skip),
-                (weight_hbm.at[:, columns(cross)], weight.at[0, own_rows]),
-                (weight_hbm.at[:, columns(tp)], weight.at[1, own_rows]),
+                (weight_hbm.at[:, columns(cross, early, width - early)], cross_weight.at[own_rows]),
+                (weight_hbm.at[:, columns(tp)], weight.at[own_rows]),
             )
         )
     ]
@@ -105,7 +115,7 @@
         return carry
 
     lax.fori_loop(0, me, greet, 0)
-    for partner in (twin, cross):
+    for partner in (twin, cross, twin_cross):
         pl.semaphore_signal(barrier, inc=1, device_id={"tp": partner}, device_id_type=MESH)
 
     step = lax.broadcasted_iota(jnp.int32, (order, SUB, LANES), 1).astype(jnp.float32)
@@ -153,7 +163,7 @@
         total = total * jnp.exp((step - float(SUB - 1)) * rates)
         own_state[:, cols] = jnp.sum(total, axis=1)
 
-    pl.semaphore_wait(barrier, n_seq - 1 - me + 2)
+    pl.semaphore_wait(barrier, n_seq - 1 - me + 3)
 
     def halo_copy(i):
         return pltpu.make_async_remote_copy(
@@ -185,24 +195,35 @@
             device_id_type=MESH,
         )
 
-    def weight_copy(i):
+    def tp_copy(i, src, dst, target):
         return pltpu.make_async_remote_copy(
-            src_ref=weight_hbm.at[:, columns((twin_cross, twin)[i])],
-            dst_ref=weight.at[i, twin_rows],
-            send_sem=twin_sem.at[i],
-            recv_sem=twin_sem.at[3 + i],
-            device_id={"tp": twin},
+            src_ref=src,
+            dst_ref=dst,
+            send_sem=tp_out.at[i],
+            recv_sem=tp_in.at[i],
+            device_id={"tp": target},
             device_id_type=MESH,
         )
 
-    hyena_copy = pltpu.make_async_remote_copy(
-        src_ref=hyena,
-        dst_ref=twin_hyena,
-        send_sem=twin_sem.at[2],
-        recv_sem=twin_sem.at[5],
-        device_id={"tp": twin},
-        device_id_type=MESH,
+    weight_copies = (
+        tp_copy(
+            0,
+            weight_hbm.at[:, columns(twin_cross, early, width - early)],
+            cross_weight.at[twin_rows],
+            twin,
+        ),
+        tp_copy(1, weight_hbm.at[:, columns(twin)], weight.at[twin_rows], twin),
+        tp_copy(2, weight_hbm.at[:, columns(cross, 0, early)], far_weight.at[own_rows], cross),
+        tp_copy(
+            3,
+            weight_hbm.at[:, columns(twin_cross, 0, early)],
+            far_weight.at[twin_rows],
+            twin_cross,
+        ),
     )
+    hyena_cross = tp_copy(4, hyena, cross_hyena, cross)
+    hyena_twin = tp_copy(5, hyena, twin_hyena, twin)
+    hyena_far = tp_copy(6, cross_hyena, far_hyena, twin)
 
     def cross_copy(c):
         return pltpu.make_async_remote_copy(
@@ -224,8 +245,8 @@
         return carry
 
     lax.fori_loop(me + 1, n_seq, send_state, 0)
-    for i in range(2):
-        weight_copy(i).start()
+    for copy in weight_copies:
+        copy.start()
 
     def local_conv(half, carry):
         cols = pl.ds(pl.multiple_of(half * LANES, LANES), LANES)
@@ -307,34 +328,52 @@
             if b < blocks - 1:
                 term = term * decay
     hyena[...] = queries[...].astype(jnp.bfloat16)
-    hyena_copy.start()
-
-    def product(rows_of, block, c, part):
-        tile = weight[block, part * channels : (part + 1) * channels, c * piece : (c + 1) * piece]
+    hyena_cross.start()
+    hyena_twin.start()
+
+    def product(rows_of, matrix, part, c):
+        tile = matrix[part * channels : (part + 1) * channels, c * piece : (c + 1) * piece]
         return jnp.dot(rows_of[...], tile, preferred_element_type=jnp.float32)
 
+    late = range(CHUNKS - EARLY)
     loads[7].wait()
-    for c in range(CHUNKS):
-        own_part[c] = product(hyena, 0, c, 0)
-    weight_copy(0).wait_recv()
-    hyena_copy.wait_recv()
-    for c in range(CHUNKS):
-        cross_send[c] = (own_part[c] + product(twin_hyena, 0, c, 1)).astype(jnp.bfloat16)
+    for c in late:
+        own_part[c] = product(hyena, cross_weight, 0, c)
+    weight_copies[0].wait_recv()
+    hyena_twin.wait_recv()
+    for c in late:
+        cross_send[c] = (own_part[c] + product(twin_hyena, cross_weight, 1, c)).astype(jnp.bfloat16)
         cross_copy(c).start()
     loads[8].wait()
-    weight_copy(1).wait_recv()
+    weight_copies[1].wait_recv()
     for c in range(CHUNKS):
-        own_part[c] = product(hyena, 1, c, 0) + product(twin_hyena, 1, c, 1)
-    for c in range(CHUNKS):
+        own_part[c] = product(hyena, weight, 0, c) + product(twin_hyena, weight, 1, c)
+    hyena_cross.wait_recv()
+    hyena_far.start()
+    weight_copies[2].wait_recv()
+    for c in range(EARLY):
+        own_part[c] = own_part[c] + product(cross_hyena, far_weight, 0, c)
+    hyena_far.wait_recv()
+    weight_copies[3].wait_recv()
+
+    def result_copy(c):
+        cols = slice(c * piece, (c + 1) * piece)
+        return pltpu.make_async_copy(result.at[c], out_hbm.at[:, cols], result_sem.at[c])
+
+    for c in range(EARLY):
+        total = own_part[c] + product(far_hyena, far_weight, 1, c)
+        result[c] = total.astype(jnp.bfloat16)
+        result_copy(c).start()
+    for c in late:
         cross_copy(c).wait_recv()
-        total = own_part[c] + cross_recv[c].astype(jnp.float32)
-        out_ref[:, c * piece : (c + 1) * piece] = total.astype(out_ref.dtype)
-
-    for c in range(CHUNKS):
+        total = own_part[EARLY + c] + cross_recv[c].astype(jnp.float32)
+        result[EARLY + c] = total.astype(jnp.bfloat16)
+        result_copy(EARLY + c).start()
+
+    for c in late:
         cross_copy(c).wait_send()
-    for i in range(2):
-        weight_copy(i).wait_send()
-    hyena_copy.wait_send()
+    for copy in weight_copies + (hyena_cross, hyena_twin, hyena_far):
+        copy.wait_send()
 
     @pl.when(me < n_seq - 1)
     def _():
@@ -347,6 +386,8 @@
         return carry
 
     lax.fori_loop(me + 1, n_seq, sent, 0)
+    for c in range(CHUNKS):
+        result_copy(c).wait()
 
 
 def solution(mesh):
@@ -359,19 +400,20 @@
         width = out_weight.shape[1] // n_tp
         piece = width // CHUNKS
         f32, bf16 = jnp.float32, jnp.bfloat16
-        pieces = pltpu.VMEM((CHUNKS, rows, piece), bf16)
         return pl.pallas_call(
             functools.partial(kernel, n_seq, n_tp),
             out_shape=jax.ShapeDtypeStruct((rows, width), bf16),
             in_specs=[pl.BlockSpec(memory_space=pltpu.HBM)] * 8,
-            out_specs=pl.BlockSpec(memory_space=pltpu.VMEM),
+            out_specs=pl.BlockSpec(memory_space=pl.ANY),
             scratch_shapes=[
                 pltpu.VMEM((3, rows, channels), bf16),
                 pltpu.VMEM((3, n_taps, channels), f32),
                 pltpu.VMEM((order, channels), f32),
                 pltpu.VMEM((order, channels), f32),
                 pltpu.VMEM((1, channels), f32),
-                pltpu.VMEM((2, 2 * channels, width), bf16),
+                pltpu.VMEM((2 * channels, width), bf16),
+                pltpu.VMEM((2 * channels, width - EARLY * piece), bf16),
+                pltpu.VMEM((2 * channels, EARLY * piece), bf16),
                 pltpu.VMEM((3, EDGE, channels), bf16),
                 pltpu.VMEM((3, rows + SUB, channels), f32),
                 pltpu.VMEM((rows + SUB, channels), f32),
@@ -384,8 +426,11 @@
                 pltpu.VMEM((rows, channels), f32),
                 pltpu.VMEM((rows, channels), bf16),
                 pltpu.VMEM((rows, channels), bf16),
-                pieces,
-                pieces,
+                pltpu.VMEM((rows, channels), bf16),
+                pltpu.VMEM((rows, channels), bf16),
+                pltpu.VMEM((CHUNKS, rows, piece), bf16),
+                pltpu.VMEM((CHUNKS - EARLY, rows, piece), bf16),
+                pltpu.VMEM((CHUNKS - EARLY, rows, piece), bf16),
                 pltpu.VMEM((CHUNKS, rows, piece), f32),
                 pltpu.SemaphoreType.DMA((9,)),
                 pltpu.SemaphoreType.DMA((6,)),
@@ -393,8 +438,10 @@
                 pltpu.SemaphoreType.DMA((n_seq,)),
                 pltpu.SemaphoreType.DMA((n_seq,)),
                 pltpu.SemaphoreType.DMA((n_seq,)),
-                pltpu.SemaphoreType.DMA((6,)),
-                pltpu.SemaphoreType.DMA((CHUNKS,)),
+                pltpu.SemaphoreType.DMA((7,)),
+                pltpu.SemaphoreType.DMA((7,)),
+                pltpu.SemaphoreType.DMA((CHUNKS - EARLY,)),
+                pltpu.SemaphoreType.DMA((CHUNKS - EARLY,)),
                 pltpu.SemaphoreType.DMA((CHUNKS,)),
             ],
             compiler_params=pltpu.CompilerParams(

time: 22.7 us -> 26.7 us (1.18)
  the two profiles are of different devices: /device:TPU:9 before, /device:TPU:0 now
where the time goes in v3:
time: 26.7 us; the launch traced here: 26.5 us
  Pallas kernels  24.8 us (93%)
  local copies, waits for them, and re-layouts  1.67 us (6%)
    pallas_call x1, Pallas kernels, local(): pl.pallas_call(functools.partial(kernel, n_seq, n_tp), out_shape=jax.Shap...  24.8 us
    unnamed x1, local copies, waits for them, and re-layouts  1.67 us

profile of v3, /device:TPU:0, one launch (start us, length us, event | category | flops | bytes accessed | tf_op | source)
XLA Modules:
  0.0 26.5 jit_solution(2003808899704460474)
XLA Ops:
  0.0 24.8 %shard_map.82 = bf16[128,1024]{1,0:T(8,128)(2,1)} custom-call(bf16[128,256]{1,0:T(8,128)(2,1)} %query_hbm.1, bf16[128,256]{1,0:T(8,128)(2,1)} %key_hbm.1, bf16[128,256]{1,0:T(8,128)(2,1)} %value_hbm.1, f32[3,7,256]{2,1,0:T(8,128)} %taps_hbm.1, f32[16,256]{1,0:T(8,128)} %residue_hbm.1, f32[16,256]{1,0:T(8,128)} %rate_hbm.1, f32[1,256]{1,0:T(1,128)} %bitcast.1, ...), custom_call_target="tpu_custom_call" | custom-call | tf_op jit(solution)/shard_map/pallas_call | solution.py:403
  24.8 1.7 %copy.10 = bf16[128,1024]{1,0:T(8,128)(2,1)} copy(bf16[128,1024]{1,0:T(8,128)(2,1)} %shard_map.82) | data formatting | bytes 524288

commit v4 on v2

--- a/solution.py
+++ b/solution.py
@@ -30,7 +30,7 @@
     rate_hbm,
     skip_hbm,
     weight_hbm,
-    out_ref,
+    out_hbm,
     streams,
     taps,
     residue,
@@ -49,6 +49,7 @@
     queries,
     hyena,
     twin_hyena,
+    result,
     cross_send,
     cross_recv,
     own_part,
@@ -61,13 +62,14 @@
     twin_sem,
     cross_out,
     cross_in,
+    result_sem,
 ):
     rows, channels = query_hbm.shape
     order = rate_hbm.shape[0]
     n_taps = taps_hbm.shape[1]
     blocks = rows // SUB
     halves = channels // LANES
-    width = out_ref.shape[1]
+    width = out_hbm.shape[1]
     piece = width // CHUNKS
     me = lax.axis_index("seq")
     tp = lax.axis_index("tp")
@@ -151,7 +153,7 @@
         for b in range(2, blocks):
             total = total * decay + gext[(b + 1) * SUB : (b + 2) * SUB, cols][None]
         total = total * jnp.exp((step - float(SUB - 1)) * rates)
-        own_state[:, cols] = jnp.sum(total, axis=1)
+        own_state[:, cols] = jnp.sum(total, axis=1).astype(jnp.bfloat16)
 
     pl.semaphore_wait(barrier, n_seq - 1 - me + 2)
 
@@ -219,11 +221,11 @@
         for i in (1, 2, 0):
             halo_copy(i).start()
 
-    def send_state(d, carry):
-        state_copy(me, d).start()
+    def send_state(i, carry):
+        state_copy(me, n_seq - 1 - i).start()
         return carry
 
-    lax.fori_loop(me + 1, n_seq, send_state, 0)
+    lax.fori_loop(0, n_seq - 1 - me, send_state, 0)
     for i in range(2):
         weight_copy(i).start()
 
@@ -256,20 +258,21 @@
     for i in range(3):
         extended[i, 0:SUB] = halo[i].astype(jnp.float32)[EDGE - SUB :]
     head = short_conv(1, 0, SUB) * short_conv(2, 0, SUB)
-    own_head[...] = head
+    stacked = jnp.concatenate([head[:, cols] for cols in lanes], axis=0)
+    own_head[...] = stacked.astype(jnp.bfloat16)
     gext[SUB : 2 * SUB] = head
 
-    def send_head(d, carry):
-        head_copy(me, d).start()
+    def send_head(i, carry):
+        head_copy(me, n_seq - 1 - i).start()
         return carry
 
-    lax.fori_loop(me + 1, n_seq, send_head, 0)
+    lax.fori_loop(0, n_seq - 1 - me, send_head, 0)
 
     queries[...] = short_conv(0, 0, rows)
     for cols in lanes:
         total = conv[:, cols]
         for j in range(SUB):
-            total = total + own_head[j : j + 1, cols] * fext[SUB - j : SUB - j + rows, cols]
+            total = total + gext[SUB + j : SUB + j + 1, cols] * fext[SUB - j : SUB - j + rows, cols]
         conv[:, cols] = total
 
     loads[6].wait()
@@ -280,7 +283,11 @@
         held, front = carry
         state_copy(d, d).wait_recv()
         head_copy(d, d).wait_recv()
-        return held * spans + states[d], front * wide + heads[d][None]
+        stacked = heads[d].astype(jnp.float32)
+        head = jnp.concatenate(
+            [stacked[half * SUB : (half + 1) * SUB] for half in range(halves)], axis=1
+        )
+        return held * spans + states[d].astype(jnp.float32), front * wide + head[None]
 
     held, front = lax.fori_loop(
         0,
@@ -325,10 +332,15 @@
     weight_copy(1).wait_recv()
     for c in range(CHUNKS):
         own_part[c] = product(hyena, 1, c, 0) + product(twin_hyena, 1, c, 1)
+    def result_copy(c):
+        cols = slice(c * piece, (c + 1) * piece)
+        return pltpu.make_async_copy(result.at[c], out_hbm.at[:, cols], result_sem.at[c])
+
     for c in range(CHUNKS):
         cross_copy(c).wait_recv()
         total = own_part[c] + cross_recv[c].astype(jnp.float32)
-        out_ref[:, c * piece : (c + 1) * piece] = total.astype(out_ref.dtype)
+        result[c] = total.astype(jnp.bfloat16)
+        result_copy(c).start()
 
     for c in range(CHUNKS):
         cross_copy(c).wait_send()
@@ -347,6 +359,8 @@
         return carry
 
     lax.fori_loop(me + 1, n_seq, sent, 0)
+    for c in range(CHUNKS):
+        result_copy(c).wait()
 
 
 def solution(mesh):
@@ -364,7 +378,7 @@
             functools.partial(kernel, n_seq, n_tp),
             out_shape=jax.ShapeDtypeStruct((rows, width), bf16),
             in_specs=[pl.BlockSpec(memory_space=pltpu.HBM)] * 8,
-            out_specs=pl.BlockSpec(memory_space=pltpu.VMEM),
+            out_specs=pl.BlockSpec(memory_space=pl.ANY),
             scratch_shapes=[
                 pltpu.VMEM((3, rows, channels), bf16),
                 pltpu.VMEM((3, n_taps, channels), f32),
@@ -377,13 +391,14 @@
                 pltpu.VMEM((rows + SUB, channels), f32),
                 pltpu.VMEM((rows + SUB, channels), f32),
                 pltpu.VMEM((rows, channels), f32),
-                pltpu.VMEM((n_seq, order, channels), f32),
-                pltpu.VMEM((order, channels), f32),
-                pltpu.VMEM((n_seq, SUB, channels), f32),
-                pltpu.VMEM((SUB, channels), f32),
+                pltpu.VMEM((n_seq, order, channels), bf16),
+                pltpu.VMEM((order, channels), bf16),
+                pltpu.VMEM((n_seq, SUB * channels // LANES, LANES), bf16),
+                pltpu.VMEM((SUB * channels // LANES, LANES), bf16),
                 pltpu.VMEM((rows, channels), f32),
                 pltpu.VMEM((rows, channels), bf16),
                 pltpu.VMEM((rows, channels), bf16),
+                pieces,
                 pieces,
                 pieces,
                 pltpu.VMEM((CHUNKS, rows, piece), f32),
@@ -394,6 +409,7 @@
                 pltpu.SemaphoreType.DMA((n_seq,)),
                 pltpu.SemaphoreType.DMA((n_seq,)),
                 pltpu.SemaphoreType.DMA((6,)),
+                pltpu.SemaphoreType.DMA((CHUNKS,)),
                 pltpu.SemaphoreType.DMA((CHUNKS,)),
                 pltpu.SemaphoreType.DMA((CHUNKS,)),
             ],

time: 22.7 us -> 22.5 us (level); the launches traced: 22.2 us -> 22.3 us
  no operation moved by 1% of the time
where the time goes in v4:
time: 22.5 us; the launch traced here: 22.3 us
  Pallas kernels  20.6 us (92%)
  local copies, waits for them, and re-layouts  1.67 us (7%)
    pallas_call x1, Pallas kernels, local(): pl.pallas_call(functools.partial(kernel, n_seq, n_tp), out_shape=jax.Shap...  20.6 us
    unnamed x1, local copies, waits for them, and re-layouts  1.67 us

profile of v4, /device:TPU:9, one launch (start us, length us, event | category | flops | bytes accessed | tf_op | source)
XLA Modules:
  0.0 22.3 jit_solution(2562570658944716326)
XLA Ops:
  0.0 20.6 %shard_map.82 = bf16[128,1024]{1,0:T(8,128)(2,1)} custom-call(bf16[128,256]{1,0:T(8,128)(2,1)} %query_hbm.1, bf16[128,256]{1,0:T(8,128)(2,1)} %key_hbm.1, bf16[128,256]{1,0:T(8,128)(2,1)} %value_hbm.1, f32[3,7,256]{2,1,0:T(8,128)} %taps_hbm.1, f32[16,256]{1,0:T(8,128)} %residue_hbm.1, f32[16,256]{1,0:T(8,128)} %rate_hbm.1, f32[1,256]{1,0:T(1,128)} %bitcast.1, ...), custom_call_target="tpu_custom_call" | custom-call | tf_op jit(solution)/shard_map/pallas_call | solution.py:377
  20.6 1.7 %copy.10 = bf16[128,1024]{1,0:T(8,128)(2,1)} copy(bf16[128,1024]{1,0:T(8,128)(2,1)} %shard_map.82) | data formatting | bytes 524288

commit v5 on v4

--- a/solution.py
+++ b/solution.py
@@ -40,12 +40,10 @@
     halo,
     extended,
     gext,
-    fext,
+    filt,
     conv,
     states,
     own_state,
-    heads,
-    own_head,
     queries,
     hyena,
     twin_hyena,
@@ -57,8 +55,6 @@
     halo_sem,
     state_send,
     state_recv,
-    head_send,
-    head_recv,
     twin_sem,
     cross_out,
     cross_in,
@@ -85,11 +81,11 @@
         pltpu.make_async_copy(src, dst, local_sem.at[i])
         for i, (src, dst) in enumerate(
             (
-                (rate_hbm, rate),
-                (residue_hbm, residue),
                 (key_hbm, streams.at[1]),
                 (value_hbm, streams.at[2]),
                 (taps_hbm, taps),
+                (rate_hbm, rate),
+                (residue_hbm, residue),
                 (query_hbm, streams.at[0]),
                 (skip_hbm, skip),
                 (weight_hbm.at[:, columns(cross)], weight.at[0, own_rows]),
@@ -119,47 +115,11 @@
     def amplitude_of(cols):
         return residue[:, cols] * jnp.sqrt(one_minus_exp_neg(2.0 * rate[:, cols]))
 
-    for load in loads[:2]:
-        load.wait()
-    fext[0:SUB] = jnp.zeros((SUB, channels), jnp.float32)
-    for cols in lanes:
-        rates = cube(rate[:, cols])
-        decay = jnp.exp(-float(SUB) * rates)
-        term = cube(amplitude_of(cols)) * jnp.exp(-step * rates)
-        for b in range(blocks):
-            fext[(b + 1) * SUB : (b + 2) * SUB, cols] = jnp.sum(term, axis=0)
-            if b < blocks - 1:
-                term = term * decay
-
-    for load in loads[2:6]:
-        load.wait()
-
-    def short_conv(i, first, count):
-        total = jnp.zeros((count, channels), jnp.float32)
-        for t in range(n_taps):
-            begin = first + SUB - t
-            total = total + taps[i, t : t + 1, :] * extended[i, begin : begin + count]
-        return total
-
-    for i in range(3):
-        extended[i, SUB:] = streams[i].astype(jnp.float32)
-    gext[0 : 2 * SUB] = jnp.zeros((2 * SUB, channels), jnp.float32)
-    gext[2 * SUB :] = short_conv(1, SUB, rows - SUB) * short_conv(2, SUB, rows - SUB)
-
-    for cols in lanes:
-        rates = cube(rate[:, cols])
-        decay = jnp.exp(-float(SUB) * rates)
-        total = jnp.broadcast_to(gext[2 * SUB : 3 * SUB, cols][None], (order, SUB, LANES))
-        for b in range(2, blocks):
-            total = total * decay + gext[(b + 1) * SUB : (b + 2) * SUB, cols][None]
-        total = total * jnp.exp((step - float(SUB - 1)) * rates)
-        own_state[:, cols] = jnp.sum(total, axis=1).astype(jnp.bfloat16)
-
     pl.semaphore_wait(barrier, n_seq - 1 - me + 2)
 
     def halo_copy(i):
         return pltpu.make_async_remote_copy(
-            src_ref=streams.at[i, pl.ds(rows - EDGE, EDGE)],
+            src_ref=(query_hbm, key_hbm, value_hbm)[i].at[pl.ds(rows - EDGE, EDGE)],
             dst_ref=halo.at[i],
             send_sem=halo_sem.at[i],
             recv_sem=halo_sem.at[3 + i],
@@ -177,16 +137,6 @@
             device_id_type=MESH,
         )
 
-    def head_copy(slot, d):
-        return pltpu.make_async_remote_copy(
-            src_ref=own_head,
-            dst_ref=heads.at[slot],
-            send_sem=head_send.at[d],
-            recv_sem=head_recv.at[slot],
-            device_id={"seq": d},
-            device_id_type=MESH,
-        )
-
     def weight_copy(i):
         return pltpu.make_async_remote_copy(
             src_ref=weight_hbm.at[:, columns((twin_cross, twin)[i])],
@@ -221,6 +171,44 @@
         for i in (1, 2, 0):
             halo_copy(i).start()
 
+    def short_conv(i, first, count):
+        total = jnp.zeros((count, channels), jnp.float32)
+        for t in range(n_taps):
+            begin = first + SUB - t
+            total = total + taps[i, t : t + 1, :] * extended[i, begin : begin + count]
+        return total
+
+    for load in loads[:3]:
+        load.wait()
+    gext[0:SUB] = jnp.zeros((SUB, channels), jnp.float32)
+    for i in (1, 2):
+        extended[i, SUB:] = streams[i].astype(jnp.float32)
+    gext[2 * SUB :] = short_conv(1, SUB, rows - SUB) * short_conv(2, SUB, rows - SUB)
+
+    @pl.when(me == 0)
+    def _():
+        halo[...] = jnp.zeros_like(halo)
+
+    @pl.when(me > 0)
+    def _():
+        for i in (1, 2, 0):
+            halo_copy(i).wait_recv()
+
+    for i in range(3):
+        extended[i, 0:SUB] = halo[i].astype(jnp.float32)[EDGE - SUB :]
+    gext[SUB : 2 * SUB] = short_conv(1, 0, SUB) * short_conv(2, 0, SUB)
+
+    for load in loads[3:5]:
+        load.wait()
+    for cols in lanes:
+        rates = cube(rate[:, cols])
+        decay = jnp.exp(-float(SUB) * rates)
+        total = jnp.broadcast_to(gext[SUB : 2 * SUB, cols][None], (order, SUB, LANES))
+        for b in range(1, blocks):
+            total = total * decay + gext[(b + 1) * SUB : (b + 2) * SUB, cols][None]
+        total = total * jnp.exp((step - float(SUB - 1)) * rates)
+        own_state[:, cols] = jnp.sum(total, axis=1).astype(jnp.bfloat16)
+
     def send_state(i, carry):
         state_copy(me, n_seq - 1 - i).start()
         return carry
@@ -228,6 +216,15 @@
     lax.fori_loop(0, n_seq - 1 - me, send_state, 0)
     for i in range(2):
         weight_copy(i).start()
+
+    for cols in lanes:
+        rates = cube(rate[:, cols])
+        decay = jnp.exp(-float(SUB) * rates)
+        term = cube(amplitude_of(cols)) * jnp.exp(-step * rates)
+        for b in range(blocks):
+            filt[b * SUB : (b + 1) * SUB, cols] = jnp.sum(term, axis=0)
+            if b < blocks - 1:
+                term = term * decay
 
     def local_conv(half, carry):
         cols = pl.ds(pl.multiple_of(half * LANES, LANES), LANES)
@@ -235,7 +232,7 @@
         for s in range(SUB):
             shifted = gext[SUB - s : SUB - s + rows, cols]
             for q in range(blocks):
-                tap = fext[(q + 1) * SUB + s : (q + 1) * SUB + s + 1, cols]
+                tap = filt[q * SUB + s : q * SUB + s + 1, cols]
                 if q == 0:
                     total = total + tap * shifted
                 else:
@@ -246,65 +243,23 @@
 
     lax.fori_loop(0, halves, local_conv, 0)
 
-    @pl.when(me == 0)
-    def _():
-        halo[...] = jnp.zeros_like(halo)
-
-    @pl.when(me > 0)
-    def _():
-        for i in (1, 2, 0):
-            halo_copy(i).wait_recv()
-
-    for i in range(3):
-        extended[i, 0:SUB] = halo[i].astype(jnp.float32)[EDGE - SUB :]
-    head = short_conv(1, 0, SUB) * short_conv(2, 0, SUB)
-    stacked = jnp.concatenate([head[:, cols] for cols in lanes], axis=0)
-    own_head[...] = stacked.astype(jnp.bfloat16)
-    gext[SUB : 2 * SUB] = head
-
-    def send_head(i, carry):
-        head_copy(me, n_seq - 1 - i).start()
-        return carry
-
-    lax.fori_loop(0, n_seq - 1 - me, send_head, 0)
-
+    loads[5].wait()
+    extended[0, SUB:] = streams[0].astype(jnp.float32)
     queries[...] = short_conv(0, 0, rows)
-    for cols in lanes:
-        total = conv[:, cols]
-        for j in range(SUB):
-            total = total + gext[SUB + j : SUB + j + 1, cols] * fext[SUB - j : SUB - j + rows, cols]
-        conv[:, cols] = total
 
     loads[6].wait()
     spans = jnp.exp(-float(rows) * rate[...])
-    wide = jnp.broadcast_to(spans[:, None, :], (order, SUB, channels))
-
-    def take_state(d, carry):
-        held, front = carry
+
+    def take_state(d, held):
         state_copy(d, d).wait_recv()
-        head_copy(d, d).wait_recv()
-        stacked = heads[d].astype(jnp.float32)
-        head = jnp.concatenate(
-            [stacked[half * SUB : (half + 1) * SUB] for half in range(halves)], axis=1
-        )
-        return held * spans + states[d].astype(jnp.float32), front * wide + head[None]
-
-    held, front = lax.fori_loop(
-        0,
-        me,
-        take_state,
-        (
-            jnp.zeros((order, channels), jnp.float32),
-            jnp.zeros((order, SUB, channels), jnp.float32),
-        ),
-    )
+        return held * spans + states[d].astype(jnp.float32)
+
+    held = lax.fori_loop(0, me, take_state, jnp.zeros((order, channels), jnp.float32))
 
     for cols in lanes:
         rates = cube(rate[:, cols])
         decay = jnp.exp(-float(SUB) * rates)
-        ahead = jnp.exp((step - float(rows - 1)) * rates) * front[:, :, cols]
-        carried = amplitude_of(cols) * (held[:, cols] + jnp.sum(ahead, axis=1))
-        term = cube(carried) * jnp.exp(-(step + 1.0) * rates)
+        term = cube(amplitude_of(cols) * held[:, cols]) * jnp.exp(-(step + 1.0) * rates)
         direct = skip[:, cols]
         for b in range(blocks):
             here = slice(b * SUB, (b + 1) * SUB)
@@ -355,7 +310,6 @@
 
     def sent(d, carry):
         state_copy(me, d).wait_send()
-        head_copy(me, d).wait_send()
         return carry
 
     lax.fori_loop(me + 1, n_seq, sent, 0)
@@ -389,12 +343,10 @@
                 pltpu.VMEM((3, EDGE, channels), bf16),
                 pltpu.VMEM((3, rows + SUB, channels), f32),
                 pltpu.VMEM((rows + SUB, channels), f32),
-                pltpu.VMEM((rows + SUB, channels), f32),
+                pltpu.VMEM((rows, channels), f32),
                 pltpu.VMEM((rows, channels), f32),
                 pltpu.VMEM((n_seq, order, channels), bf16),
                 pltpu.VMEM((order, channels), bf16),
-                pltpu.VMEM((n_seq, SUB * channels // LANES, LANES), bf16),
-                pltpu.VMEM((SUB * channels // LANES, LANES), bf16),
                 pltpu.VMEM((rows, channels), f32),
                 pltpu.VMEM((rows, channels), bf16),
                 pltpu.VMEM((rows, channels), bf16),
@@ -404,8 +356,6 @@
                 pltpu.VMEM((CHUNKS, rows, piece), f32),
                 pltpu.SemaphoreType.DMA((9,)),
                 pltpu.SemaphoreType.DMA((6,)),
-                pltpu.SemaphoreType.DMA((n_seq,)),
-                pltpu.SemaphoreType.DMA((n_seq,)),
                 pltpu.SemaphoreType.DMA((n_seq,)),
                 pltpu.SemaphoreType.DMA((n_seq,)),
                 pltpu.SemaphoreType.DMA((6,)),

time: 22.5 us -> 22.9 us (1.018)
  Pallas kernels: 20.6 us -> 21 us
    pallas_call x1, Pallas kernels: 20.6 us -> 21 us  [local(): pl.pallas_call(functools.partial(kernel, n_seq, n_tp), out_shape=jax.Shap...]
where the time goes in v5:
time: 22.9 us; the launch traced here: 22.7 us
  Pallas kernels  21 us (92%)
  local copies, waits for them, and re-layouts  1.67 us (7%)
    pallas_call x1, Pallas kernels, local(): pl.pallas_call(functools.partial(kernel, n_seq, n_tp), out_shape=jax.Shap...  21 us
    unnamed x1, local copies, waits for them, and re-layouts  1.67 us

profile of v5, /device:TPU:9, one launch (start us, length us, event | category | flops | bytes accessed | tf_op | source)
XLA Modules:
  0.0 22.7 jit_solution(9881482450546946469)
XLA Ops:
  0.0 21.0 %shard_map.82 = bf16[128,1024]{1,0:T(8,128)(2,1)} custom-call(bf16[128,256]{1,0:T(8,128)(2,1)} %query_hbm.1, bf16[128,256]{1,0:T(8,128)(2,1)} %key_hbm.1, bf16[128,256]{1,0:T(8,128)(2,1)} %value_hbm.1, f32[3,7,256]{2,1,0:T(8,128)} %taps_hbm.1, f32[16,256]{1,0:T(8,128)} %residue_hbm.1, f32[16,256]{1,0:T(8,128)} %rate_hbm.1, f32[1,256]{1,0:T(1,128)} %bitcast.1, ...), custom_call_target="tpu_custom_call" | custom-call | tf_op jit(solution)/shard_map/pallas_call | solution.py:331
  21.1 1.7 %copy.10 = bf16[128,1024]{1,0:T(8,128)(2,1)} copy(bf16[128,1024]{1,0:T(8,128)(2,1)} %shard_map.82) | data formatting | bytes 524288

commit v6 on v4

--- a/solution.py
+++ b/solution.py
@@ -30,7 +30,7 @@
     rate_hbm,
     skip_hbm,
     weight_hbm,
-    out_hbm,
+    out_ref,
     streams,
     taps,
     residue,
@@ -49,7 +49,6 @@
     queries,
     hyena,
     twin_hyena,
-    result,
     cross_send,
     cross_recv,
     own_part,
@@ -62,14 +61,13 @@
     twin_sem,
     cross_out,
     cross_in,
-    result_sem,
 ):
     rows, channels = query_hbm.shape
     order = rate_hbm.shape[0]
     n_taps = taps_hbm.shape[1]
     blocks = rows // SUB
     halves = channels // LANES
-    width = out_hbm.shape[1]
+    width = out_ref.shape[1]
     piece = width // CHUNKS
     me = lax.axis_index("seq")
     tp = lax.axis_index("tp")
@@ -332,15 +330,10 @@
     weight_copy(1).wait_recv()
     for c in range(CHUNKS):
         own_part[c] = product(hyena, 1, c, 0) + product(twin_hyena, 1, c, 1)
-    def result_copy(c):
-        cols = slice(c * piece, (c + 1) * piece)
-        return pltpu.make_async_copy(result.at[c], out_hbm.at[:, cols], result_sem.at[c])
-
     for c in range(CHUNKS):
         cross_copy(c).wait_recv()
         total = own_part[c] + cross_recv[c].astype(jnp.float32)
-        result[c] = total.astype(jnp.bfloat16)
-        result_copy(c).start()
+        out_ref[:, c * piece : (c + 1) * piece] = total.astype(out_ref.dtype)
 
     for c in range(CHUNKS):
         cross_copy(c).wait_send()
@@ -359,8 +352,6 @@
         return carry
 
     lax.fori_loop(me + 1, n_seq, sent, 0)
-    for c in range(CHUNKS):
-        result_copy(c).wait()
 
 
 def solution(mesh):
@@ -374,11 +365,21 @@
         piece = width // CHUNKS
         f32, bf16 = jnp.float32, jnp.bfloat16
         pieces = pltpu.VMEM((CHUNKS, rows, piece), bf16)
+        operands = (
+            query_in,
+            key_in,
+            value_in,
+            short_weight,
+            residue,
+            rate,
+            skip.reshape(1, channels),
+            out_weight,
+        )
         return pl.pallas_call(
             functools.partial(kernel, n_seq, n_tp),
             out_shape=jax.ShapeDtypeStruct((rows, width), bf16),
             in_specs=[pl.BlockSpec(memory_space=pltpu.HBM)] * 8,
-            out_specs=pl.BlockSpec(memory_space=pl.ANY),
+            out_specs=pl.BlockSpec(memory_space=pltpu.VMEM),
             scratch_shapes=[
                 pltpu.VMEM((3, rows, channels), bf16),
                 pltpu.VMEM((3, n_taps, channels), f32),
@@ -400,7 +401,6 @@
                 pltpu.VMEM((rows, channels), bf16),
                 pieces,
                 pieces,
-                pieces,
                 pltpu.VMEM((CHUNKS, rows, piece), f32),
                 pltpu.SemaphoreType.DMA((9,)),
                 pltpu.SemaphoreType.DMA((6,)),
@@ -411,20 +411,12 @@
                 pltpu.SemaphoreType.DMA((6,)),
                 pltpu.SemaphoreType.DMA((CHUNKS,)),
                 pltpu.SemaphoreType.DMA((CHUNKS,)),
-                pltpu.SemaphoreType.DMA((CHUNKS,)),
             ],
             compiler_params=pltpu.CompilerParams(
-                collective_id=0, has_side_effects=True, vmem_limit_bytes=60 * 1024 * 1024
+                collective_id=0, has_side_effects=True, vmem_limit_bytes=40 * 1024 * 1024
             ),
         )(
-            query_in,
-            key_in,
-            value_in,
-            short_weight,
-            residue,
-            rate,
-            skip.reshape(1, channels),
-            out_weight,
+            *[pltpu.with_memory_space_constraint(x, pltpu.HBM) for x in operands]
         )
 
     in_specs = (

time: 22.5 us -> 20.9 us (0.929)
  local copies, waits for them, and re-layouts: 1.67 us -> 0.71 us
  Pallas kernels: 20.6 us -> 20 us
    unnamed x1, local copies, waits for them, and re-layouts: 1.67 us -> 0.71 us
    pallas_call x1, Pallas kernels: 20.6 us -> 20 us  [local(): pl.pallas_call(functools.partial(kernel, n_seq, n_tp), out_shape=jax.Shap...]
where the time goes in v6:
time: 20.9 us; the launch traced here: 20.7 us
  Pallas kernels  20 us (96%)
  local copies, waits for them, and re-layouts  0.71 us (3%)
    pallas_call x1, Pallas kernels, local(): pl.pallas_call(functools.partial(kernel, n_seq, n_tp), out_shape=jax.Shap...  20 us
    unnamed x1, local copies, waits for them, and re-layouts  0.71 us

profile of v6, /device:TPU:9, one launch (start us, length us, event | category | flops | bytes accessed | tf_op | source)
XLA Modules:
  0.0 20.7 jit_solution(11801381310057329520)
XLA Ops:
  0.0 20.0 %shard_map.82 = bf16[128,1024]{1,0:T(8,128)(2,1)S(1)} custom-call(bf16[128,256]{1,0:T(8,128)(2,1)} %query_hbm.1, bf16[128,256]{1,0:T(8,128)(2,1)} %key_hbm.1, bf16[128,256]{1,0:T(8,128)(2,1)} %value_hbm.1, f32[3,7,256]{2,1,0:T(8,128)} %taps_hbm.1, f32[16,256]{1,0:T(8,128)} %residue_hbm.1, f32[16,256]{1,0:T(8,128)} %rate_hbm.1, f32[1,256]{1,0:T(1,128)} %bitcast.1, ...), custom_call_target="tpu_custom_call" | custom-call | tf_op jit(solution)/shard_map/pallas_call | solution.py:378
  20.0 0.7 %copy.10 = bf16[128,1024]{1,0:T(8,128)(2,1)} copy(bf16[128,1024]{1,0:T(8,128)(2,1)S(1)} %shard_map.82) | data formatting | bytes 524288

commit v7 on v3

--- a/solution.py
+++ b/solution.py
@@ -12,7 +12,7 @@
 SUB = 8
 EDGE = 16
 CHUNKS = 4
-EARLY = 2
+EARLY = 1
 
 
 def one_minus_exp_neg(x):
@@ -31,7 +31,7 @@
     rate_hbm,
     skip_hbm,
     weight_hbm,
-    out_hbm,
+    out_ref,
     streams,
     taps,
     residue,
@@ -54,7 +54,6 @@
     twin_hyena,
     cross_hyena,
     far_hyena,
-    result,
     cross_send,
     cross_recv,
     own_part,
@@ -68,14 +67,13 @@
     tp_in,
     cross_out,
     cross_in,
-    result_sem,
 ):
     rows, channels = query_hbm.shape
     order = rate_hbm.shape[0]
     n_taps = taps_hbm.shape[1]
     blocks = rows // SUB
     halves = channels // LANES
-    width = out_hbm.shape[1]
+    width = out_ref.shape[1]
     piece = width // CHUNKS
     me = lax.axis_index("seq")
     tp = lax.axis_index("tp")
@@ -161,7 +159,7 @@
         for b in range(2, blocks):
             total = total * decay + gext[(b + 1) * SUB : (b + 2) * SUB, cols][None]
         total = total * jnp.exp((step - float(SUB - 1)) * rates)
-        own_state[:, cols] = jnp.sum(total, axis=1)
+        own_state[:, cols] = jnp.sum(total, axis=1).astype(jnp.bfloat16)
 
     pl.semaphore_wait(barrier, n_seq - 1 - me + 3)
 
@@ -240,12 +238,12 @@
         for i in (1, 2, 0):
             halo_copy(i).start()
 
-    def send_state(d, carry):
-        state_copy(me, d).start()
+    def send_state(i, carry):
+        state_copy(me, n_seq - 1 - i).start()
         return carry
 
-    lax.fori_loop(me + 1, n_seq, send_state, 0)
-    for copy in weight_copies:
+    lax.fori_loop(0, n_seq - 1 - me, send_state, 0)
+    for copy in weight_copies[2:]:
         copy.start()
 
     def local_conv(half, carry):
@@ -277,20 +275,23 @@
     for i in range(3):
         extended[i, 0:SUB] = halo[i].astype(jnp.float32)[EDGE - SUB :]
     head = short_conv(1, 0, SUB) * short_conv(2, 0, SUB)
-    own_head[...] = head
+    stacked = jnp.concatenate([head[:, cols] for cols in lanes], axis=0)
+    own_head[...] = stacked.astype(jnp.bfloat16)
     gext[SUB : 2 * SUB] = head
 
-    def send_head(d, carry):
-        head_copy(me, d).start()
+    def send_head(i, carry):
+        head_copy(me, n_seq - 1 - i).start()
         return carry
 
-    lax.fori_loop(me + 1, n_seq, send_head, 0)
+    lax.fori_loop(0, n_seq - 1 - me, send_head, 0)
+    for copy in weight_copies[:2]:
+        copy.start()
 
     queries[...] = short_conv(0, 0, rows)
     for cols in lanes:
         total = conv[:, cols]
         for j in range(SUB):
-            total = total + own_head[j : j + 1, cols] * fext[SUB - j : SUB - j + rows, cols]
+            total = total + gext[SUB + j : SUB + j + 1, cols] * fext[SUB - j : SUB - j + rows, cols]
         conv[:, cols] = total
 
     loads[6].wait()
@@ -301,7 +302,11 @@
         held, front = carry
         state_copy(d, d).wait_recv()
         head_copy(d, d).wait_recv()
-        return held * spans + states[d], front * wide + heads[d][None]
+        stacked = heads[d].astype(jnp.float32)
+        head = jnp.concatenate(
+            [stacked[half * SUB : (half + 1) * SUB] for half in range(halves)], axis=1
+        )
+        return held * spans + states[d].astype(jnp.float32), front * wide + head[None]
 
     held, front = lax.fori_loop(
         0,
@@ -344,31 +349,24 @@
     for c in late:
         cross_send[c] = (own_part[c] + product(twin_hyena, cross_weight, 1, c)).astype(jnp.bfloat16)
         cross_copy(c).start()
+    hyena_cross.wait_recv()
+    hyena_far.start()
     loads[8].wait()
     weight_copies[1].wait_recv()
     for c in range(CHUNKS):
         own_part[c] = product(hyena, weight, 0, c) + product(twin_hyena, weight, 1, c)
-    hyena_cross.wait_recv()
-    hyena_far.start()
     weight_copies[2].wait_recv()
     for c in range(EARLY):
         own_part[c] = own_part[c] + product(cross_hyena, far_weight, 0, c)
     hyena_far.wait_recv()
     weight_copies[3].wait_recv()
-
-    def result_copy(c):
-        cols = slice(c * piece, (c + 1) * piece)
-        return pltpu.make_async_copy(result.at[c], out_hbm.at[:, cols], result_sem.at[c])
-
     for c in range(EARLY):
         total = own_part[c] + product(far_hyena, far_weight, 1, c)
-        result[c] = total.astype(jnp.bfloat16)
-        result_copy(c).start()
+        out_ref[:, c * piece : (c + 1) * piece] = total.astype(out_ref.dtype)
     for c in late:
         cross_copy(c).wait_recv()
         total = own_part[EARLY + c] + cross_recv[c].astype(jnp.float32)
-        result[EARLY + c] = total.astype(jnp.bfloat16)
-        result_copy(EARLY + c).start()
+        out_ref[:, early + c * piece : early + (c + 1) * piece] = total.astype(out_ref.dtype)
 
     for c in late:
         cross_copy(c).wait_send()
@@ -386,8 +384,6 @@
         return carry
 
     lax.fori_loop(me + 1, n_seq, sent, 0)
-    for c in range(CHUNKS):
-        result_copy(c).wait()
 
 
 def solution(mesh):
@@ -400,11 +396,22 @@
         width = out_weight.shape[1] // n_tp
         piece = width // CHUNKS
         f32, bf16 = jnp.float32, jnp.bfloat16
+        pieces = pltpu.VMEM((CHUNKS - EARLY, rows, piece), bf16)
+        operands = (
+            query_in,
+            key_in,
+            value_in,
+            short_weight,
+            residue,
+            rate,
+            skip.reshape(1, channels),
+            out_weight,
+        )
         return pl.pallas_call(
             functools.partial(kernel, n_seq, n_tp),
             out_shape=jax.ShapeDtypeStruct((rows, width), bf16),
             in_specs=[pl.BlockSpec(memory_space=pltpu.HBM)] * 8,
-            out_specs=pl.BlockSpec(memory_space=pl.ANY),
+            out_specs=pl.BlockSpec(memory_space=pltpu.VMEM),
             scratch_shapes=[
                 pltpu.VMEM((3, rows, channels), bf16),
                 pltpu.VMEM((3, n_taps, channels), f32),
@@ -419,18 +426,17 @@
                 pltpu.VMEM((rows + SUB, channels), f32),
                 pltpu.VMEM((rows + SUB, channels), f32),
                 pltpu.VMEM((rows, channels), f32),
-                pltpu.VMEM((n_seq, order, channels), f32),
-                pltpu.VMEM((order, channels), f32),
-                pltpu.VMEM((n_seq, SUB, channels), f32),
-                pltpu.VMEM((SUB, channels), f32),
+                pltpu.VMEM((n_seq, order, channels), bf16),
+                pltpu.VMEM((order, channels), bf16),
+                pltpu.VMEM((n_seq, SUB * channels // LANES, LANES), bf16),
+                pltpu.VMEM((SUB * channels // LANES, LANES), bf16),
                 pltpu.VMEM((rows, channels), f32),
                 pltpu.VMEM((rows, channels), bf16),
                 pltpu.VMEM((rows, channels), bf16),
                 pltpu.VMEM((rows, channels), bf16),
                 pltpu.VMEM((rows, channels), bf16),
-                pltpu.VMEM((CHUNKS, rows, piece), bf16),
-                pltpu.VMEM((CHUNKS - EARLY, rows, piece), bf16),
-                pltpu.VMEM((CHUNKS - EARLY, rows, piece), bf16),
+                pieces,
+                pieces,
                 pltpu.VMEM((CHUNKS, rows, piece), f32),
                 pltpu.SemaphoreType.DMA((9,)),
                 pltpu.SemaphoreType.DMA((6,)),
@@ -442,20 +448,12 @@
                 pltpu.SemaphoreType.DMA((7,)),
                 pltpu.SemaphoreType.DMA((CHUNKS - EARLY,)),
                 pltpu.SemaphoreType.DMA((CHUNKS - EARLY,)),
-                pltpu.SemaphoreType.DMA((CHUNKS,)),
             ],
             compiler_params=pltpu.CompilerParams(
-                collective_id=0, has_side_effects=True, vmem_limit_bytes=60 * 1024 * 1024
+                collective_id=0, has_side_effects=True, vmem_limit_bytes=40 * 1024 * 1024
             ),
         )(
-            query_in,
-            key_in,
-            value_in,
-            short_weight,
-            residue,
-            rate,
-            skip.reshape(1, channels),
-            out_weight,
+            *[pltpu.with_memory_space_constraint(x, pltpu.HBM) for x in operands]
         )
 
     in_specs = (

time: 26.7 us -> 21 us (0.79)
  Pallas kernels: 24.8 us -> 20 us
  local copies, waits for them, and re-layouts: 1.67 us -> 0.71 us
    pallas_call x1, Pallas kernels: 24.8 us -> 20 us  [local(): pl.pallas_call(functools.partial(kernel, n_seq, n_tp), out_shape=jax.Shap...]
    unnamed x1, local copies, waits for them, and re-layouts: 1.67 us -> 0.71 us
where the time goes in v7:
time: 21 us; the launch traced here: 20.7 us
  Pallas kernels  20 us (95%)
  local copies, waits for them, and re-layouts  0.71 us (3%)
    pallas_call x1, Pallas kernels, local(): pl.pallas_call(functools.partial(kernel, n_seq, n_tp), out_shape=jax.Shap...  20 us
    unnamed x1, local copies, waits for them, and re-layouts  0.71 us

profile of v7, /device:TPU:0, one launch (start us, length us, event | category | flops | bytes accessed | tf_op | source)
XLA Modules:
  0.0 20.7 jit_solution(9714940435624824070)
XLA Ops:
  0.0 20.0 %shard_map.82 = bf16[128,1024]{1,0:T(8,128)(2,1)S(1)} custom-call(bf16[128,256]{1,0:T(8,128)(2,1)} %query_hbm.1, bf16[128,256]{1,0:T(8,128)(2,1)} %key_hbm.1, bf16[128,256]{1,0:T(8,128)(2,1)} %value_hbm.1, f32[3,7,256]{2,1,0:T(8,128)} %taps_hbm.1, f32[16,256]{1,0:T(8,128)} %residue_hbm.1, f32[16,256]{1,0:T(8,128)} %rate_hbm.1, f32[1,256]{1,0:T(1,128)} %bitcast.1, ...), custom_call_target="tpu_custom_call" | custom-call | tf_op jit(solution)/shard_map/pallas_call | solution.py:410
  20.0 0.7 %copy.10 = bf16[128,1024]{1,0:T(8,128)(2,1)} copy(bf16[128,1024]{1,0:T(8,128)(2,1)S(1)} %shard_map.82) | data formatting | bytes 524288

commit v8 on v7

--- a/solution.py
+++ b/solution.py
@@ -98,7 +98,7 @@
                 (taps_hbm, taps),
                 (query_hbm, streams.at[0]),
                 (skip_hbm, skip),
-                (weight_hbm.at[:, columns(cross, early, width - early)], cross_weight.at[own_rows]),
+                (weight_hbm.at[:, columns(cross)], cross_weight.at[own_rows]),
                 (weight_hbm.at[:, columns(tp)], weight.at[own_rows]),
             )
         )
@@ -206,7 +206,7 @@
     weight_copies = (
         tp_copy(
             0,
-            weight_hbm.at[:, columns(twin_cross, early, width - early)],
+            weight_hbm.at[:, columns(twin_cross)],
             cross_weight.at[twin_rows],
             twin,
         ),
@@ -243,8 +243,11 @@
         return carry
 
     lax.fori_loop(0, n_seq - 1 - me, send_state, 0)
-    for copy in weight_copies[2:]:
-        copy.start()
+    @pl.when(me > 0)
+    def _():
+        for copy in weight_copies[2:]:
+            copy.start()
+
 
     def local_conv(half, carry):
         cols = pl.ds(pl.multiple_of(half * LANES, LANES), LANES)
@@ -333,44 +336,78 @@
             if b < blocks - 1:
                 term = term * decay
     hyena[...] = queries[...].astype(jnp.bfloat16)
-    hyena_cross.start()
+    @pl.when(me > 0)
+    def _():
+        hyena_cross.start()
+
     hyena_twin.start()
 
     def product(rows_of, matrix, part, c):
         tile = matrix[part * channels : (part + 1) * channels, c * piece : (c + 1) * piece]
         return jnp.dot(rows_of[...], tile, preferred_element_type=jnp.float32)
 
-    late = range(CHUNKS - EARLY)
+    def send_cross(c):
+        total = own_part[c] + product(twin_hyena, cross_weight, 1, c)
+        cross_send[c] = total.astype(jnp.bfloat16)
+        cross_copy(c).start()
+
+    def finish(c, total):
+        out_ref[:, c * piece : (c + 1) * piece] = total.astype(out_ref.dtype)
+
+    def finish_cross(c):
+        cross_copy(c).wait_recv()
+        finish(c, own_part[c] + cross_recv[c].astype(jnp.float32))
+
+    late = range(EARLY, CHUNKS)
     loads[7].wait()
-    for c in late:
+    for c in range(CHUNKS):
         own_part[c] = product(hyena, cross_weight, 0, c)
     weight_copies[0].wait_recv()
     hyena_twin.wait_recv()
     for c in late:
-        cross_send[c] = (own_part[c] + product(twin_hyena, cross_weight, 1, c)).astype(jnp.bfloat16)
-        cross_copy(c).start()
-    hyena_cross.wait_recv()
-    hyena_far.start()
+        send_cross(c)
+
+    @pl.when(me == 0)
+    def _():
+        for c in range(EARLY):
+            send_cross(c)
+
+    @pl.when(me > 0)
+    def _():
+        hyena_cross.wait_recv()
+        hyena_far.start()
+
     loads[8].wait()
     weight_copies[1].wait_recv()
     for c in range(CHUNKS):
         own_part[c] = product(hyena, weight, 0, c) + product(twin_hyena, weight, 1, c)
-    weight_copies[2].wait_recv()
-    for c in range(EARLY):
-        own_part[c] = own_part[c] + product(cross_hyena, far_weight, 0, c)
-    hyena_far.wait_recv()
-    weight_copies[3].wait_recv()
-    for c in range(EARLY):
-        total = own_part[c] + product(far_hyena, far_weight, 1, c)
-        out_ref[:, c * piece : (c + 1) * piece] = total.astype(out_ref.dtype)
+
+    @pl.when(me > 0)
+    def _():
+        weight_copies[2].wait_recv()
+        hyena_far.wait_recv()
+        weight_copies[3].wait_recv()
+        for c in range(EARLY):
+            gathered = product(cross_hyena, far_weight, 0, c) + product(far_hyena, far_weight, 1, c)
+            finish(c, own_part[c] + gathered)
+
     for c in late:
-        cross_copy(c).wait_recv()
-        total = own_part[EARLY + c] + cross_recv[c].astype(jnp.float32)
-        out_ref[:, early + c * piece : early + (c + 1) * piece] = total.astype(out_ref.dtype)
+        finish_cross(c)
+
+    @pl.when(me == 0)
+    def _():
+        for c in range(EARLY):
+            finish_cross(c)
+            cross_copy(c).wait_send()
+
+    @pl.when(me > 0)
+    def _():
+        for copy in weight_copies[2:] + (hyena_cross, hyena_far):
+            copy.wait_send()
 
     for c in late:
         cross_copy(c).wait_send()
-    for copy in weight_copies + (hyena_cross, hyena_twin, hyena_far):
+    for copy in weight_copies[:2] + (hyena_twin,):
         copy.wait_send()
 
     @pl.when(me < n_seq - 1)
@@ -396,7 +433,7 @@
         width = out_weight.shape[1] // n_tp
         piece = width // CHUNKS
         f32, bf16 = jnp.float32, jnp.bfloat16
-        pieces = pltpu.VMEM((CHUNKS - EARLY, rows, piece), bf16)
+        pieces = pltpu.VMEM((CHUNKS, rows, piece), bf16)
         operands = (
             query_in,
             key_in,
@@ -419,7 +456,7 @@
                 pltpu.VMEM((order, channels), f32),
                 pltpu.VMEM((1, channels), f32),
                 pltpu.VMEM((2 * channels, width), bf16),
-                pltpu.VMEM((2 * channels, width - EARLY * piece), bf16),
+                pltpu.VMEM((2 * channels, width), bf16),
                 pltpu.VMEM((2 * channels, EARLY * piece), bf16),
                 pltpu.VMEM((3, EDGE, channels), bf16),
                 pltpu.VMEM((3, rows + SUB, channels), f32),
@@ -446,8 +483,8 @@
                 pltpu.SemaphoreType.DMA((n_seq,)),
                 pltpu.SemaphoreType.DMA((7,)),
                 pltpu.SemaphoreType.DMA((7,)),
-                pltpu.SemaphoreType.DMA((CHUNKS - EARLY,)),
-                pltpu.SemaphoreType.DMA((CHUNKS - EARLY,)),
+                pltpu.SemaphoreType.DMA((CHUNKS,)),
+                pltpu.SemaphoreType.DMA((CHUNKS,)),
             ],
             compiler_params=pltpu.CompilerParams(
                 collective_id=0, has_side_effects=True, vmem_limit_bytes=40 * 1024 * 1024

time: 21 us -> 20.3 us (0.967)
  the two profiles are of different devices: /device:TPU:0 before, /device:TPU:9 now
where the time goes in v8:
time: 20.3 us; the launch traced here: 20.1 us
  Pallas kernels  19.3 us (95%)
  local copies, waits for them, and re-layouts  0.71 us (3%)
    pallas_call x1, Pallas kernels, local(): pl.pallas_call(functools.partial(kernel, n_seq, n_tp), out_shape=jax.Shap...  19.3 us
    unnamed x1, local copies, waits for them, and re-layouts  0.71 us

profile of v8, /device:TPU:9, one launch (start us, length us, event | category | flops | bytes accessed | tf_op | source)
XLA Modules:
  0.0 20.1 jit_solution(5532021206158338754)
XLA Ops:
  0.0 19.3 %shard_map.82 = bf16[128,1024]{1,0:T(8,128)(2,1)S(1)} custom-call(bf16[128,256]{1,0:T(8,128)(2,1)} %query_hbm.1, bf16[128,256]{1,0:T(8,128)(2,1)} %key_hbm.1, bf16[128,256]{1,0:T(8,128)(2,1)} %value_hbm.1, f32[3,7,256]{2,1,0:T(8,128)} %taps_hbm.1, f32[16,256]{1,0:T(8,128)} %residue_hbm.1, f32[16,256]{1,0:T(8,128)} %rate_hbm.1, f32[1,256]{1,0:T(1,128)} %bitcast.1, ...), custom_call_target="tpu_custom_call" | custom-call | tf_op jit(solution)/shard_map/pallas_call | solution.py:447
  19.4 0.7 %copy.10 = bf16[128,1024]{1,0:T(8,128)(2,1)} copy(bf16[128,1024]{1,0:T(8,128)(2,1)S(1)} %shard_map.82) | data formatting | bytes 524288

commit v9 on v8

--- a/solution.py
+++ b/solution.py
@@ -11,8 +11,8 @@
 LANES = 128
 SUB = 8
 EDGE = 16
-CHUNKS = 4
-EARLY = 1
+CHUNKS = 8
+EARLY = 2
 
 
 def one_minus_exp_neg(x):

time: 20.3 us -> 20.4 us (level)
  no operation moved by 1% of the time
where the time goes in v9:
time: 20.4 us; the launch traced here: 20.1 us
  Pallas kernels  19.4 us (95%)
  local copies, waits for them, and re-layouts  0.71 us (3%)
    pallas_call x1, Pallas kernels, local(): pl.pallas_call(functools.partial(kernel, n_seq, n_tp), out_shape=jax.Shap...  19.4 us
    unnamed x1, local copies, waits for them, and re-layouts  0.71 us

profile of v9, /device:TPU:9, one launch (start us, length us, event | category | flops | bytes accessed | tf_op | source)
XLA Modules:
  0.0 20.1 jit_solution(1448773701456106055)
XLA Ops:
  0.0 19.4 %shard_map.82 = bf16[128,1024]{1,0:T(8,128)(2,1)S(1)} custom-call(bf16[128,256]{1,0:T(8,128)(2,1)} %query_hbm.1, bf16[128,256]{1,0:T(8,128)(2,1)} %key_hbm.1, bf16[128,256]{1,0:T(8,128)(2,1)} %value_hbm.1, f32[3,7,256]{2,1,0:T(8,128)} %taps_hbm.1, f32[16,256]{1,0:T(8,128)} %residue_hbm.1, f32[16,256]{1,0:T(8,128)} %rate_hbm.1, f32[1,256]{1,0:T(1,128)} %bitcast.1, ...), custom_call_target="tpu_custom_call" | custom-call | tf_op jit(solution)/shard_map/pallas_call | solution.py:447
  19.4 0.7 %copy.10 = bf16[128,1024]{1,0:T(8,128)(2,1)} copy(bf16[128,1024]{1,0:T(8,128)(2,1)S(1)} %shard_map.82) | data formatting | bytes 524288
